TPU v7x, 128 devices: a whole 4x4x4 slice. The times are simulated.
128 devices in a mesh: blk: 32 (over y_lo, z, x), uly: 4 (over y_hi, core).
Axes of the slice: x: 4, y: 4 (y_hi: 2, y_lo: 2; y = y_hi * 2 + y_lo), z: 4, core: 2. Of those that a mesh axis runs over, the one named last changes fastest.
Arguments:
- tokens: bfloat16 [2, 8192, 1536], P(None, ('blk', 'uly')), may hold values from -6 to 6
- cotangent: bfloat16 [2, 8192, 1536], P(None, ('blk', 'uly')), may hold values from -6 to 6
- lengths: int32 [2], replicated, may hold values from 4097 to 8192, as said below
- set_index: int32 [2], replicated, may hold values from 0 to 7
- norm_in: float32 [1536], replicated, may hold values from 0.25 to 1.75
- norm_ff: float32 [1536], replicated, may hold values from 0.25 to 1.75
- qkv_bias: float32 [2048], replicated, may hold values from -3 to 3
- w_qkv: bfloat16 [1536, 2048], P(('blk', 'uly')), may hold values from -0.15625 to 0.15625
- w_out: bfloat16 [1536, 1536], P(('blk', 'uly')), may hold values from -2.5 to 2.5
- w_gate_up: bfloat16 [2, 1536, 8960], P(None, 'blk', 'uly'), may hold values from -0.15625 to 0.15625
- w_down: bfloat16 [8960, 1536], P('uly', 'blk'), may hold values from -0.0625 to 0.0625
- a_wide: bfloat16 [6, 8, 16, 1536], replicated, may hold values from -0.15625 to 0.15625
- a_down: bfloat16 [8, 16, 8960], replicated, may hold values from -0.0625 to 0.0625
- b_wide: bfloat16 [3, 8, 16, 1536], replicated, may hold values from -1.5 to 1.5
- b_kv: bfloat16 [2, 8, 16, 256], replicated, may hold values from -1.5 to 1.5
- b_ff: bfloat16 [2, 8, 16, 8960], replicated, may hold values from -1.5 to 1.5
Outputs:
- result_tokens: bfloat16 [2, 8192, 1536], P(None, ('blk', 'uly'))
- input_grad: float32 [2, 8192, 1536], P(None, ('blk', 'uly'))
- grad_a_wide: float32 [6, 8, 16, 1536], replicated
- grad_a_down: float32 [8, 16, 8960], replicated
- grad_b_wide: float32 [3, 8, 16, 1536], replicated
- grad_b_kv: float32 [2, 8, 16, 256], replicated
- grad_b_ff: float32 [2, 8, 16, 8960], replicated
Inputs may be any that keep to these rules, and one draw needn't show every extreme that they name: Each sequence's valid slots are its first lengths[s]; one sequence, drawn from the seed, fills all 8192 slots.
All inputs are finite; a program needn't handle non-finite values.
Results may differ from a plain program's by a relative error of at most 0.024.
Values may be sent and summed in bfloat16 or wider, within the bound.
A program may use at most 320 MiB of HBM per device.

v0:
```python
import functools

import jax
import jax.numpy as jnp
import numpy as np
from jax import lax
from jax.experimental import pallas as pl
from jax.experimental.pallas import tpu as pltpu
from jax.sharding import PartitionSpec as P

HEADS = 12
KV_HEADS = 2
HEAD = 128
GROUP = HEADS // KV_HEADS
FF = 8960
SETS = 8
D = 1536
CHUNK = 128
CHUNKS = 64
PADDED = 2304
EPS = 1e-06
THETA = 1000000.0
LOG2E = 1.4426950408889634
LN2 = 0.6931471805599453
MESH = pl.DeviceIdType.MESH
BF = jnp.bfloat16
F32 = jnp.float32
ANY = pl.BlockSpec(memory_space=pltpu.HBM)
IN_VMEM = pl.BlockSpec(memory_space=pltpu.VMEM)
HELD = pltpu.HBM


def blk_of(y, z, x):
    return y * 16 + z * 4 + x


def low_chunk(blk):
    return (1 - blk // 16) * 2 * blk + blk // 16 * (63 - 2 * blk)


def place():
    blk = lax.axis_index("blk")
    return blk // 16, (blk // 4) % 4, blk % 4, blk, lax.axis_index("uly")


def ring_others():
    y, z, x, blk, uly = place()
    return [
        (blk_of(1 - y, z, x), uly),
        (blk_of(y, z, (x + 1) % 4), uly),
        (blk_of(y, z, (x + 3) % 4), uly),
        (blk_of(y, (z + 1) % 4, x), uly),
        (blk_of(y, (z + 3) % 4, x), uly),
    ]


def choose(number, value):
    chosen = value(0)
    for c in range(1, SETS):
        chosen = jnp.where(number == c, value(c), chosen)
    return chosen


def gain(ref, first):
    return jnp.concatenate([ref[n : n + 1, :] for n in range(first, first + D // 128)], axis=1)


def greet(others, meanwhile=None):
    barrier = pltpu.get_barrier_semaphore()
    for other in others:
        pl.semaphore_signal(barrier, inc=1, device_id=other, device_id_type=MESH)
    if meanwhile is not None:
        meanwhile()
    pl.semaphore_wait(barrier, len(others))


class Gather:
    sends = 31

    def __init__(self, src, dst, send_sem, recv_sem, local_sem, orders=(0, 1)):
        self.src, self.dst, self.orders = src, dst, orders
        self.streams = range(len(orders))
        self.send_sem, self.recv_sem, self.local_sem = send_sem, recv_sem, local_sem
        self.y, self.z, self.x, self.blk, self.uly = place()
        self.count = [0] * len(orders)
        self.sent = []
        self.local = []

    def at(self, stream, y, p, q):
        order = self.orders[stream]
        return blk_of(y, order * p + (1 - order) * q, order * q + (1 - order) * p)

    def pq(self, stream):
        order = self.orders[stream]
        return (
            order * self.z + (1 - order) * self.x,
            order * self.x + (1 - order) * self.z,
        )

    def send(self, stream, item, target, src=None):
        copy = pltpu.make_async_remote_copy(
            src_ref=self.dst(stream, item) if src is None else src,
            dst_ref=self.dst(stream, item),
            send_sem=self.send_sem.at[stream, self.count[stream]],
            recv_sem=self.recv_sem.at[stream, item],
            device_id=(target, self.uly),
            device_id_type=MESH,
        )
        self.count[stream] += 1
        copy.start()
        self.sent.append(copy)

    def wait(self, stream, item):
        ref = self.dst(stream, item)
        pltpu.make_async_remote_copy(
            src_ref=ref,
            dst_ref=ref,
            send_sem=self.send_sem.at[stream, 0],
            recv_sem=self.recv_sem.at[stream, item],
            device_id=(self.blk, self.uly),
            device_id_type=MESH,
        ).wait_recv()

    def start(self):
        for s in self.streams:
            p, q = self.pq(s)
            self.send(s, self.blk, self.at(s, 1 - self.y, p, q), self.src(s))
        for s in self.streams:
            p, q = self.pq(s)
            for d in (1, 3):
                self.send(s, self.blk, self.at(s, self.y, (p + d) % 4, q), self.src(s))
            copy = pltpu.make_async_copy(self.src(s), self.dst(s, self.blk), self.local_sem.at[s])
            copy.start()
            self.local.append(copy)

    def second(self):
        for s in self.streams:
            p, q = self.pq(s)
            item = self.at(s, 1 - self.y, p, q)
            self.wait(s, item)
            for d in (1, 3):
                self.send(s, item, self.at(s, self.y, (p + d) % 4, q))
            for d in (1, 3):
                onward = self.at(s, self.y, p, (q + d) % 4)
                self.send(s, self.blk, onward, self.src(s))
                self.send(s, item, onward)

    def spread(self, s, item):
        p, q = self.pq(s)
        for d in (1, 3):
            self.send(s, item, self.at(s, self.y, p, (q + d) % 4))

    def third(self):
        for k, y in enumerate((self.y, 1 - self.y)):
            for s in self.streams:
                p, q = self.pq(s)
                for d in (3, 1):
                    item = self.at(s, y, (p + d) % 4, q)
                    self.wait(s, item)
                    if (d == 3) == (k == 0):
                        self.send(s, item, self.at(s, self.y, (p + 4 - d) % 4, q))
                    self.spread(s, item)
        for y in (self.y, 1 - self.y):
            for s in self.streams:
                p, q = self.pq(s)
                item = self.at(s, y, (p + 2) % 4, q)
                self.wait(s, item)
                self.spread(s, item)

    def fourth(self):
        for e in (0, 1, 3, 2):
            for k, y in enumerate((self.y, 1 - self.y)):
                for s in self.streams:
                    p, q = self.pq(s)
                    for d in (3, 1):
                        item = self.at(s, y, (p + e) % 4, (q + d) % 4)
                        self.wait(s, item)
                        if (d == 3) == (k == 0):
                            self.send(s, item, self.at(s, self.y, p, (q + 4 - d) % 4))

    def last(self):
        for e in (0, 1, 3, 2):
            for y in (self.y, 1 - self.y):
                for s in self.streams:
                    p, q = self.pq(s)
                    self.wait(s, self.at(s, y, (p + e) % 4, (q + 2) % 4))
        for copy in self.local:
            copy.wait()
        for copy in self.sent:
            copy.wait_send()


GATHER_SEMS = lambda *lead: [
    pltpu.SemaphoreType.DMA(lead + (2, Gather.sends)),
    pltpu.SemaphoreType.DMA(lead + (2, 32)),
    pltpu.SemaphoreType.DMA(lead + (2,)),
]


KEYS = 1024
KEYS_BACK = 512
ROWS = GROUP * CHUNK


def head_columns(ref, slot):
    return jnp.concatenate(
        [
            ref[slot * CHUNK : (slot + 1) * CHUNK, n * HEAD : (n + 1) * HEAD].T
            for n in range(GROUP)
        ],
        axis=1,
    )


def head_rows(ref, slot):
    return jnp.concatenate(
        [
            ref[slot * CHUNK : (slot + 1) * CHUNK, n * HEAD : (n + 1) * HEAD]
            for n in range(GROUP)
        ],
        axis=0,
    )


def key_block(kv_ref, step, keys):
    count = keys // CHUNK
    rows = kv_ref[pl.ds(step * count, count)].reshape(keys, 2 * HEAD)
    return rows[:, :HEAD], rows[:, HEAD:]


def dot(a, b):
    return jnp.dot(a, b, preferred_element_type=F32)


def key_places(step, keys):
    return lax.broadcasted_iota(jnp.int32, (keys, ROWS), 0) + step * keys


def dot_nt(a, b):
    return lax.dot_general(a, b, (((1,), (1,)), ((), ())), preferred_element_type=F32)


def forward_blocks(slot, first, last, turned_ref, kv_ref, limit_ref, acc_ref, stat_ref):
    turned = turned_ref[slot]
    limit = limit_ref[slot, 0:1, :]

    def step(n, carry):
        top, total = carry
        keys, values = key_block(kv_ref, n, KEYS)
        scores = jnp.where(key_places(n, KEYS) <= limit, dot(keys, turned), -1e30)
        new_top = jnp.maximum(top, jnp.max(scores, axis=0, keepdims=True))
        fade = jnp.exp2(top - new_top)
        probs = jnp.exp2(scores - new_top)
        total = total * fade + jnp.sum(probs, axis=0, keepdims=True)
        acc_ref[slot] = acc_ref[slot] * fade + dot(values.T, probs.astype(BF))
        return new_top, total

    top, total = lax.fori_loop(
        first, last, step, (stat_ref[slot, 0, 0:1, :], stat_ref[slot, 1, 0:1, :])
    )
    stat_ref[slot, 0, 0:1, :] = top
    stat_ref[slot, 1, 0:1, :] = total


def forward_end(slot, mixed_ref, lse_ref, acc_ref, stat_ref):
    top, total = stat_ref[slot, 0, 0:1, :], stat_ref[slot, 1, 0:1, :]
    out = acc_ref[slot] / total
    for n in range(GROUP):
        mixed_ref[slot * CHUNK : (slot + 1) * CHUNK, n * HEAD : (n + 1) * HEAD] = out[
            :, n * CHUNK : (n + 1) * CHUNK
        ].T.astype(BF)
    lse_ref[slot] = jnp.broadcast_to(top + jnp.log2(total), (8, ROWS))


def uly_others():
    y, z, x, blk, uly = place()
    return [(blk, (uly + 2) % 4), (blk, uly + 1 - 2 * (uly % 2)), (blk, 3 - uly)]


def ring_place(w):
    y, z, x, blk, uly = place()
    return (blk_of(w % 2, z, x), (w // 2) * 2 + uly % 2)


def ring_at():
    y, z, x, blk, uly = place()
    return (uly // 2) * 2 + y


def wait_arrival(ref, sem):
    pltpu.make_async_copy(ref, ref, sem).wait()


def remote(src, dst, send, recv, device):
    return pltpu.make_async_remote_copy(
        src_ref=src, dst_ref=dst, send_sem=send, recv_sem=recv, device_id=device, device_id_type=MESH
    )


class Deliver:
    def __init__(self):
        self.sent = []

    def send(self, src, dst, send, recv, device):
        y, z, x, blk, uly = place()
        here = jnp.logical_and(device[0] == blk, device[1] == uly)

        @pl.when(here)
        def _():
            pltpu.make_async_copy(src, dst, recv).start()

        @pl.when(jnp.logical_not(here))
        def _():
            remote(src, dst, send, recv, device).start()

        self.sent.append((here, src, dst, send, recv, device))

    def end(self):
        for here, *copy in self.sent:

            @pl.when(jnp.logical_not(here))
            def _():
                remote(*copy).wait_send()


class Ring:
    sends = 15

    def __init__(self, src, dst, y, order, way, send_sem, recv_sem):
        self.src, self.dst, self.y, self.order, self.way = src, dst, y, order, way
        self.send_sem, self.recv_sem = send_sem, recv_sem
        self.own_y, self.z, self.x, self.blk, self.uly = place()
        self.p = order * self.z + (1 - order) * self.x
        self.q = order * self.x + (1 - order) * self.z
        self.sent = []

    def at(self, y, p, q):
        order = self.order
        return blk_of(y, order * p + (1 - order) * q, order * q + (1 - order) * p)

    def index(self, p, q):
        return self.at(0, p, q)

    def send(self, p, q, dp, dq, src=None):
        ref = self.dst(self.at(self.y, p, q))
        target = self.at(self.own_y, (self.p + dp) % 4, (self.q + dq) % 4)
        copy = remote(
            ref if src is None else src, ref, self.send_sem.at[len(self.sent)],
            self.recv_sem.at[self.index(p, q)], (target, self.uly),
        )
        copy.start()
        self.sent.append(copy)

    def wait(self, p, q):
        wait_arrival(self.dst(self.at(self.y, p, q)), self.recv_sem.at[self.index(p, q)])

    def start(self):
        for d in (1, 3):
            self.send(self.p, self.q, d, 0, self.src)

    def second(self):
        for d in (4 - self.way, self.way):
            p = (self.p + d) % 4
            self.wait(p, self.q)
            if d == 4 - self.way:
                self.send(p, self.q, self.way, 0)

    def third(self):
        self.wait((self.p + 2) % 4, self.q)

    def spread(self, e):
        p = (self.p + e) % 4
        for d in (1, 3):
            self.send(p, self.q, 0, d, self.src if e == 0 else None)

    def fourth(self, e):
        p = (self.p + e) % 4
        for d in (4 - self.way, self.way):
            q = (self.q + d) % 4
            self.wait(p, q)
            if d == 4 - self.way:
                self.send(p, q, 0, self.way)

    def last(self):
        for e in (0, 1, 3, 2):
            self.wait((self.p + e) % 4, (self.q + 2) % 4)
        for copy in self.sent:
            copy.wait_send()


class Spread:
    def __init__(self, own, all_ref, send_sem, recv_sem, local_sem):
        self.own, self.all_ref = own, all_ref
        self.send_sem, self.recv_sem, self.local_sem = send_sem, recv_sem, local_sem
        self.w = ring_at()
        self.core = lax.axis_index("uly") % 2
        self.sibling = uly_others()[1]
        self.sent = []

    def piece(self, d, rows=slice(None), core=None):
        core = self.core if core is None else core
        ref = self.all_ref.at[core, (self.w + d) % 4]
        return ref if rows == slice(None) else ref.at[pl.ds(rows.start, rows.stop - rows.start)]

    def send(self, src, dst, recv, device):
        copy = remote(src, dst, self.send_sem.at[len(self.sent)], self.recv_sem.at[recv], device)
        copy.start()
        self.sent.append(copy)

    def pair(self, d, src=None):
        self.send(self.piece(d) if src is None else src, self.piece(d), 4 + d, self.sibling)

    def start(self):
        self.local = pltpu.make_async_copy(self.own, self.piece(0), self.local_sem)
        self.local.start()
        self.send(self.own, self.piece(0), 0, ring_place((self.w + 1) % 4))
        self.send(self.own, self.piece(0), 1, ring_place((self.w + 3) % 4))
        self.pair(0, self.own)

    def second(self):
        half = CHUNK // 2
        wait_arrival(self.piece(3), self.recv_sem.at[0])
        low = self.piece(3, slice(0, half))
        self.send(low, low, 2, ring_place((self.w + 1) % 4))
        self.pair(3)
        wait_arrival(self.piece(1), self.recv_sem.at[1])
        high = self.piece(1, slice(half, CHUNK))
        self.send(high, high, 3, ring_place((self.w + 3) % 4))
        self.pair(1)

    def third(self):
        half = CHUNK // 2
        wait_arrival(self.piece(2, slice(0, half)), self.recv_sem.at[2])
        wait_arrival(self.piece(2, slice(half, CHUNK)), self.recv_sem.at[3])
        self.pair(2)

    def last(self):
        for d in range(4):
            wait_arrival(self.piece(d, core=1 - self.core), self.recv_sem.at[4 + d])
        for copy in self.sent:
            copy.wait_send()
        self.local.wait()


SPREAD_SEMS = [pltpu.SemaphoreType.DMA((8,)), pltpu.SemaphoreType.DMA((8,)), pltpu.SemaphoreType.DMA]
FF_COLS = PADDED // 2


def forward_kernel(
    tokens_ref, cot_ref, length_hbm, set_hbm, qkv_hbm, w_out_hbm, gate_up_hbm, down_hbm, gains_hbm, freq_hbm,
    a_hbm, b_hbm, bkv_hbm,
    q_out, mixed_out, lse_out, kv_out, wq_out, wo_out, gate_all, up_all, down_all, rows_hbm, normed_out,
    resid_out, cot_out, nf_out, cot_all, limit_out, cos_out, sin_out, b_qkv_out, ao_out, a_out, bo_out,
    q_ref, mixed_ref, lse_ref, rows_out, normed_ref, resid_ref, cot_own, limit_ref, cos_ref, sin_ref,
    b_qkv_ref, ao_ref, a_ref, b_ref, bkv_ref, a_sets, b_sets, bkv_sets, turned_ref,
    length_ref, set_ref, qkv_ref, out_ref, gate_up_ref, down_ref, gains_ref, freq_ref, kv_all, wq_all, wo_all, rows, cot_in, kv_part, acc_ref, stat_ref, qkv_in, out_in, qkv_part, out_part,
    nf_own, cross_out, cross_in, qkv_pieces, out_pieces, ff_ref,
    *sems,
):
    y, z, x, blk, uly = place()
    core, h = uly % 2, uly // 2
    sems = list(sems)

    def take(count):
        got = sems[:count]
        del sems[:count]
        return got

    chunk = 2 * blk + h
    upper = chunk // 32
    home = (1 - h) * blk + h * (31 - blk)
    row_to = [[(home, hh * 2 + s) for hh in (0, 1)] for s in (0, 1)]
    row_from = [(b, hh * 2 + half) for b, hh in ((blk, 0), (31 - blk, 1)) for half in (0, 1)]
    lower = low_chunk(blk)
    out_to = [(2 * (blk % 16) + q // 2, (blk // 16) * 2 + q % 2) for q in range(4)]
    out_from = [(16 * h + blk // 2, u) for u in range(4)]
    sibling = uly_others()[1]
    set_sem = sems.pop()
    in_sem = sems.pop()
    in_copies = [
        pltpu.make_async_copy(src, dst, in_sem.at[n])
        for n, (src, dst) in enumerate(
            (
                (qkv_hbm, qkv_ref), (w_out_hbm, out_ref), (gate_up_hbm, gate_up_ref), (down_hbm, down_ref),
                (length_hbm, length_ref), (set_hbm, set_ref), (gains_hbm, gains_ref), (freq_hbm, freq_ref),
            )
        )
    ]
    for copy in in_copies:
        copy.start()
    set_copies = [
        pltpu.make_async_copy(src, dst, set_sem.at[n])
        for n, (src, dst) in enumerate(
            ((a_hbm.at[pl.ds(0, 4)], a_sets), (b_hbm.at[pl.ds(0, 2)], b_sets), (bkv_hbm, bkv_sets))
        )
    ]
    for copy in set_copies:
        copy.start()

    def prepare():
        qkv_pieces[...] = jnp.zeros_like(qkv_pieces)
        out_pieces[...] = jnp.zeros_like(out_pieces)
        for copy in in_copies:
            copy.wait()
        group = GROUP * HEAD
        for hh in (0, 1):
            qkv_pieces[2 * hh, :12] = qkv_ref[:, hh * group : hh * group + 512]
            for place_at, start, size in (
                (0, hh * group + 512, 256),
                (256, HEADS * HEAD + hh * HEAD, HEAD),
                (384, HEADS * HEAD + 256 + hh * HEAD, HEAD),
            ):
                qkv_pieces[2 * hh + 1, :12, place_at : place_at + size] = qkv_ref[:, start : start + size]
        for q in range(4):
            out_pieces[q, :12] = out_ref[:, q * 384 : (q + 1) * 384]
        for n in range(3):
            part = (gate_up_ref[n] if n < 2 else down_ref[...]).astype(F32)
            none = jnp.zeros((48, 64), F32)
            left = jnp.concatenate([part, none], axis=1)
            right = jnp.concatenate([none, part], axis=1)
            ff_ref[n] = jnp.where(jnp.broadcast_to(core, (48, PADDED)) == 1, right, left).astype(BF)

    greet(
        ring_others() + uly_others() + [(blk_of(1 - y, z, x), (uly + 2) % 4)]
        + row_to[0] + row_to[1] + row_from + out_to + out_from,
        prepare,
    )

    length = length_ref[0] * (1 - core) + length_ref[1] * core

    deliver = Deliver()
    piece_send, piece_recv, row_send, row_recv = take(4)
    for q in range(4):
        deliver.send(qkv_pieces.at[q], qkv_in.at[uly], piece_send.at[q], piece_recv.at[uly], (blk, q))
    for q in range(4):
        deliver.send(out_pieces.at[q], out_in.at[uly], piece_send.at[4 + q], piece_recv.at[4 + uly], out_to[q])
    for s in (0, 1):
        for hh in (0, 1):
            deliver.send(
                tokens_ref.at[s], rows.at[upper, core], row_send.at[s * 2 + hh],
                row_recv.at[upper * 2 + core], row_to[s][hh],
            )

    wide = PADDED // 2
    gathered = (gate_all, up_all, down_all)
    ff_send, ff_recv, y_send, y_recv, y_local = take(5)
    other_blk = blk_of(1 - y, z, x)

    def ff_part(n, half):
        return ff_ref.at[n, :, pl.ds(pl.multiple_of(half * wide, 128), wide)]

    y_copies = []
    for n, ref in enumerate(gathered):
        copy = remote(ff_part(n, 1 - y), ref.at[blk], y_send.at[n], y_recv.at[n], (other_blk, uly))
        copy.start()
        y_copies.append(copy)
        copy = pltpu.make_async_copy(ff_part(n, y), ref.at[blk], y_local.at[n])
        copy.start()
        y_copies.append(copy)
    own_ff, other_ff = (
        [
            Ring(
                ff_part(n, y) if k == 0 else ref.at[other_blk],
                lambda item, ref=ref: ref.at[item],
                y if k == 0 else 1 - y,
                y if k == 0 else 1 - y,
                (1, 3, 1 + 2 * k)[n],
                ff_send.at[k, n], ff_recv.at[k, n],
            )
            for n, ref in enumerate(gathered)
        ]
        for k in (0, 1)
    )
    for ring in own_ff:
        ring.start()

    picked = lax.broadcasted_iota(jnp.int32, (48, 64), 1)
    picked = jnp.where(picked % 16 < 12, picked // 16 * 12 + picked % 16, -1)
    picked = jnp.where(picked == lax.broadcasted_iota(jnp.int32, (48, 64), 0), 1.0, 0.0).astype(BF)
    for u in range(4):
        wait_arrival(qkv_in.at[u], piece_recv.at[u])
    qkv_part[...] = dot(picked, qkv_in[...].reshape(64, 512)).astype(BF)
    wq = Gather(
        lambda s: qkv_part.at[:, pl.ds(256 * s, 256)],
        lambda s, item: wq_all.at[
            core, pl.ds(pl.multiple_of(item * 48, 16), 48), pl.ds(256 * s, 256)
        ],
        *take(3),
    )
    wq.start()
    for u in range(4):
        wait_arrival(out_in.at[u], piece_recv.at[4 + u])
    out_part[...] = dot(picked, out_in[...].reshape(64, 384)).astype(BF)
    for s in (0, 1):
        deliver.send(
            cot_ref.at[s], cot_in.at[core], row_send.at[4 + s], row_recv.at[4 + core], (home, upper * 2 + s)
        )

    def out_columns(item, s):
        start = ((item % 2) * 2 + core) * 384
        return pl.ds(pl.multiple_of(start + 128 * s, 128), 128 + 128 * s)

    wo = Gather(
        lambda s: out_part.at[:, pl.ds(128 * s, 128 + 128 * s)],
        lambda s, item: wo_all.at[pl.ds(pl.multiple_of((item // 2) * 48, 16), 48), out_columns(item, s)],
        *take(3),
    )
    rings = own_ff + other_ff
    def tables(slot):
        at = lower if slot == 0 else 63 - lower
        row = lax.broadcasted_iota(jnp.int32, (CHUNK, HEAD), 0) + at * CHUNK
        angle = row.astype(F32) * freq_ref[...]
        first = lax.broadcasted_iota(jnp.int32, (CHUNK, HEAD), 1) < HEAD // 2
        sine = jnp.sin(angle)
        cos_ref[slot * CHUNK : (slot + 1) * CHUNK, :] = jnp.cos(angle)
        sin_ref[slot * CHUNK : (slot + 1) * CHUNK, :] = jnp.where(first, -sine, sine)
        row = lax.broadcasted_iota(jnp.int32, (8, ROWS), 1) % CHUNK + at * CHUNK
        limit_ref[slot] = jnp.minimum(row, length - 1)

    stat_ref[:, 0] = jnp.full((2, 8, ROWS), -1e30, F32)
    stat_ref[:, 1] = jnp.zeros((2, 8, ROWS), F32)
    acc_ref[...] = jnp.zeros_like(acc_ref)
    own_set = set_ref[0] * (1 - core) + set_ref[1] * core
    for copy in set_copies:
        copy.wait()
    for sets, ref in ((a_sets, a_ref), (b_sets, b_ref), (bkv_sets, bkv_ref)):
        for n in range(ref.shape[0]):
            ref[n] = choose(own_set, lambda c: sets[n, c])
    group = GROUP * HEAD
    group_at = pl.ds(pl.multiple_of(h * group, 128), group)
    head_at = pl.ds(pl.multiple_of(h * HEAD, 128), HEAD)
    ao_ref[...] = a_ref[3, :, group_at]
    b_qkv_ref[...] = jnp.zeros_like(b_qkv_ref)
    b_qkv_ref[:16, :group] = b_ref[0, :, group_at]
    b_qkv_ref[16:32, group : group + HEAD] = bkv_ref[0, :, head_at]
    b_qkv_ref[32:, group + HEAD :] = bkv_ref[1, :, head_at]
    a_qkv = a_ref[:3].reshape(48, D)
    bo_ref = b_ref.at[1]

    def bias(n):
        at = h * GROUP + n if n < GROUP else HEADS + 2 * (n - GROUP) + h
        return gains_ref[pl.ds(2 * D_TILES + at, 1), :]

    wq.second()
    tables(0)
    wq.third()
    tables(1)
    wq.fourth()
    for n in range(3):
        y_copies[2 * n].wait_recv()
    for ring in other_ff:
        ring.start()
    for ring in rings:
        ring.spread(0)

    for n in range(4):
        wait_arrival(rows.at[n // 2, n % 2], row_recv.at[n])
        value = rows[n // 2, n % 2].astype(F32)
        at = slice(n * 64, (n + 1) * 64)
        rows_out[at, :] = rows[n // 2, n % 2]
        normed_ref[at, :] = (value * norm_scale(value) * gain(gains_ref, 0)).astype(BF)
    latent = dot_nt(normed_ref[...], a_qkv)
    adapted = dot(latent.astype(BF), b_qkv_ref[...])
    wq.last()
    pair_send, pair_recv = take(2)

    def pair_copy(ref, n):
        return remote(ref, ref, pair_send.at[n], pair_recv.at[n], sibling)

    pair_copy(wq_all.at[core], 0).start()
    wo.start()
    pair_copy(wq_all.at[core], 0).wait_send()
    pair_copy(wq_all.at[1 - core], 0).wait_recv()

    cos_table, sine_table = cos_ref[...], sin_ref[...]

    def turn(head):
        return head * cos_table + pltpu.roll(head, HEAD // 2, 1) * sine_table

    def query(n, head):
        q_ref[:, n * HEAD : (n + 1) * HEAD] = (turn(head + bias(n)) * (HEAD ** (-0.5) * LOG2E)).astype(BF)

    pairs = dot(normed_ref[...], wq_all[1, :, 256:]) + adapted[:, 768:]
    for n, head in ((0, turn(pairs[:, :HEAD] + bias(6))), (1, pairs[:, HEAD:] + bias(7))):
        at = slice(n * HEAD, (n + 1) * HEAD)
        kv_part[0, :, at] = head[:CHUNK].astype(BF)
        kv_part[1, :, at] = head[CHUNK:].astype(BF)
    kv = Gather(
        lambda s: kv_part.at[s],
        lambda s, item: kv_all.at[low_chunk(item) if s == 0 else 63 - low_chunk(item)],
        *take(3),
    )
    kv.start()
    heads = dot(normed_ref[...], wq_all[1, :, :256]) + adapted[:, 512:768]
    for n in (4, 5):
        query(n, heads[:, (n - 4) * HEAD : (n - 3) * HEAD])
    kv.second()
    for ring in rings:
        ring.second()
    wo.second()
    heads = dot(normed_ref[...], wq_all[0]) + adapted[:, :512]
    for n in range(4):
        query(n, heads[:, n * HEAD : (n + 1) * HEAD])
    kv.third()
    for ring in rings:
        ring.third()
    wo.third()
    kv.fourth()
    wo.fourth()

    for half in (0, 1):
        wait_arrival(cot_in.at[half], row_recv.at[4 + half])
        start = ((1 - h) * lower + h * (63 - lower)) * CHUNK + half * 64
        at = lax.broadcasted_iota(jnp.int32, (64, D), 0) + start
        cot_own[half * 64 : (half + 1) * 64, :] = jnp.where(
            at < length, cot_in[half].astype(F32), 0.0
        ).astype(BF)
    cot_spread = Spread(cot_own, cot_all, *take(3))
    cot_spread.start()
    kv.last()
    for e in (1, 3, 2):
        for ring in rings:
            ring.spread(e)
    (out_sem,) = take(1)
    copies = []

    def keep(*pairs):
        for src, dst in pairs:
            copies.append(pltpu.make_async_copy(src, dst, out_sem.at[len(copies)]))
            copies[-1].start()

    keep(
        (kv_all, kv_out), (wq_all, wq_out), (q_ref, q_out), (rows_out, rows_hbm), (normed_ref, normed_out),
        (cot_own, cot_out), (limit_ref, limit_out), (cos_ref, cos_out), (sin_ref, sin_out),
        (b_qkv_ref, b_qkv_out), (ao_ref, ao_out), (a_ref.at[pl.ds(0, 3)], a_out), (b_ref.at[1], bo_out),
    )
    wo.last()

    def wo_columns(c, n):
        return wo_all.at[:, pl.ds(pl.multiple_of((2 * n + c) * 384, 128), 384)]

    for n in (0, 1):
        pair_copy(wo_columns(core, n), 1 + n).start()
    for slot in (0, 1):
        turned_ref[slot] = head_columns(q_ref, slot)
    args = (turned_ref, kv_all, limit_ref, acc_ref, stat_ref)

    def end(slot):
        forward_end(slot, mixed_ref, lse_ref, acc_ref, stat_ref)

    blocks = KEYS // CHUNK
    middle = CHUNKS // 2 // blocks
    forward_blocks(0, 0, lower // blocks + 1, *args)
    forward_blocks(1, middle, (63 - lower) // blocks + 1, *args)
    end(0)
    for ring in rings:
        ring.fourth(0)
    cot_spread.second()
    forward_blocks(1, 0, middle // 2, *args)
    for ring in rings:
        ring.fourth(1)
    cot_spread.third()
    forward_blocks(1, middle // 2, middle, *args)
    end(1)
    for n in (0, 1):
        pair_copy(wo_columns(core, n), 1 + n).wait_send()
        pair_copy(wo_columns(1 - core, n), 1 + n).wait_recv()
    keep((wo_all, wo_out), (mixed_ref, mixed_out), (lse_ref, lse_out))

    def project(slot):
        mixed = mixed_ref[pl.ds(pl.multiple_of(slot * CHUNK, CHUNK), CHUNK), :]
        lifted = dot(dot_nt(mixed, ao_ref[...]).astype(BF), bo_ref[...])
        return dot(mixed, wo_all[...]) + lifted

    (cross_sem,) = take(1)
    cross_out[...] = project(1 - h).astype(BF)
    cross = remote(cross_out, cross_in, cross_sem.at[0], cross_sem.at[1], uly_others()[0])
    cross.start()
    for ring in rings:
        ring.fourth(3)
    mine = project(h) + rows_out[pl.ds(pl.multiple_of(h * CHUNK, CHUNK), CHUNK), :].astype(F32)
    for ring in rings:
        ring.fourth(2)
    cross.wait()
    residual = mine + cross_in[...].astype(F32)
    resid_ref[...] = residual
    keep((resid_ref, resid_out))
    nf_own[...] = (residual * norm_scale(residual) * gain(gains_ref, D_TILES)).astype(BF)
    keep((nf_own, nf_out))
    cot_spread.last()
    for ring in rings:
        ring.last()
    for n in range(3):
        y_copies[2 * n].wait_send()
        y_copies[2 * n + 1].wait()
    deliver.end()
    for copy in copies:
        copy.wait()


def forward(*args):
    weight = HELD((32, 48, FF_COLS), BF)
    group = GROUP * HEAD
    dma = pltpu.SemaphoreType.DMA
    spread = HELD((2, 4, CHUNK, D), BF)
    return pl.pallas_call(
        forward_kernel,
        out_shape=(
            HELD((2 * CHUNK, group), BF),
            HELD((2 * CHUNK, group), BF),
            HELD((2, 8, ROWS), F32),
            HELD((CHUNKS, CHUNK, 2 * HEAD), BF),
            HELD((2, D, 512), BF),
            HELD((D // 2, D), BF),
            weight, weight, weight,
            HELD((2 * CHUNK, D), BF),
            HELD((2 * CHUNK, D), BF),
            HELD((CHUNK, D), F32),
            HELD((CHUNK, D), BF),
            HELD((CHUNK, D), BF),
            spread,
            HELD((2, 8, ROWS), jnp.int32),
            HELD((2 * CHUNK, HEAD), F32),
            HELD((2 * CHUNK, HEAD), F32),
            HELD((48, 1024), BF),
            HELD((16, group), BF),
            HELD((3, 16, D), BF),
            HELD((16, D), BF),
        ),
        in_specs=[ANY] * 13,
        out_specs=(ANY,) * 22,
        scratch_shapes=[
            pltpu.VMEM((2 * CHUNK, group), BF),
            pltpu.VMEM((2 * CHUNK, group), BF),
            pltpu.VMEM((2, 8, ROWS), F32),
            pltpu.VMEM((2 * CHUNK, D), BF),
            pltpu.VMEM((2 * CHUNK, D), BF),
            pltpu.VMEM((CHUNK, D), F32),
            pltpu.VMEM((CHUNK, D), BF),
            pltpu.VMEM((2, 8, ROWS), jnp.int32),
            pltpu.VMEM((2 * CHUNK, HEAD), F32),
            pltpu.VMEM((2 * CHUNK, HEAD), F32),
            pltpu.VMEM((48, 1024), BF),
            pltpu.VMEM((16, group), BF),
            pltpu.VMEM((4, 16, D), BF),
            pltpu.VMEM((2, 16, D), BF),
            pltpu.VMEM((2, 16, 2 * HEAD), BF),
            pltpu.VMEM((4, SETS, 16, D), BF),
            pltpu.VMEM((2, SETS, 16, D), BF),
            pltpu.VMEM((2, SETS, 16, 2 * HEAD), BF),
            pltpu.VMEM((2, HEAD, ROWS), BF),
            pltpu.SMEM((2,), jnp.int32),
            pltpu.SMEM((2,), jnp.int32),
            pltpu.VMEM((12, 2048), BF),
            pltpu.VMEM((12, D), BF),
            pltpu.VMEM((2, 48, FF // 4), BF),
            pltpu.VMEM((48, FF // 4), BF),
            pltpu.VMEM((40, 128), F32),
            pltpu.VMEM((1, 128), F32),
            pltpu.VMEM((CHUNKS, CHUNK, 2 * HEAD), BF),
            pltpu.VMEM((2, D, 512), BF),
            pltpu.VMEM((D // 2, D), BF),
            pltpu.VMEM((2, 2, 64, D), BF),
            pltpu.VMEM((2, 64, D), BF),
            pltpu.VMEM((2, CHUNK, 2 * HEAD), BF),
            pltpu.VMEM((2, HEAD, ROWS), F32),
            pltpu.VMEM((2, 2, 8, ROWS), F32),
            pltpu.VMEM((4, 16, 512), BF),
            pltpu.VMEM((4, 16, 384), BF),
            pltpu.VMEM((48, 512), BF),
            pltpu.VMEM((48, 384), BF),
            pltpu.VMEM((CHUNK, D), BF),
            pltpu.VMEM((CHUNK, D), BF),
            pltpu.VMEM((CHUNK, D), BF),
            pltpu.VMEM((4, 16, 512), BF),
            pltpu.VMEM((4, 16, 384), BF),
            pltpu.VMEM((3, 48, PADDED), BF),
            dma((8,)), dma((8,)), dma((6,)), dma((6,)),
            dma((2, 3, Ring.sends)), dma((2, 3, 16)), dma((3,)), dma((3,)), dma((3,)),
        ]
        + GATHER_SEMS()
        + GATHER_SEMS()
        + [dma((3,)), dma((3,))]
        + GATHER_SEMS()
        + SPREAD_SEMS
        + [dma((18,)), dma((2,)), dma((8,)), dma((3,))],
        compiler_params=pltpu.CompilerParams(
            collective_id=1, has_side_effects=True, vmem_limit_bytes=48 * 2**20
        ),
        name="forward",
    )(*args)


class RingSum:
    @staticmethod
    def scratch():
        piece, half = (CHUNK, D), (CHUNK // 2, D)
        return [
            pltpu.VMEM((2,) + half, BF),
            pltpu.VMEM((2,) + piece, BF),
            pltpu.VMEM(piece, BF),
            pltpu.VMEM((2,) + piece, BF),
            pltpu.SemaphoreType.DMA((4,)),
            pltpu.SemaphoreType.DMA((4,)),
        ]

    scratches = 6

    def __init__(self, term, scratch):
        self.term = term
        self.halves, self.last_in, self.far, self.near, self.send_sem, self.recv_sem = scratch
        self.w = ring_at()
        self.sent = []

    def send(self, src, dst, recv, d):
        copy = remote(
            src, dst, self.send_sem.at[recv], self.recv_sem.at[recv], ring_place((self.w + d) % 4)
        )
        copy.start()
        self.sent.append(copy)

    def first(self):
        half = CHUNK // 2
        self.far[...] = self.term(2).astype(BF)
        self.send(self.far.at[pl.ds(0, half)], self.halves.at[0], 0, 1)
        self.send(self.far.at[pl.ds(half, half)], self.halves.at[1], 1, 3)

    def second(self):
        half = CHUNK // 2
        for k, d in ((0, 1), (1, 3)):
            total = self.term(d)
            wait_arrival(self.halves.at[k], self.recv_sem.at[k])
            rows = slice(k * half, (k + 1) * half)
            other = slice((1 - k) * half, (2 - k) * half)
            self.near[k, rows] = (total[rows] + self.halves[k].astype(F32)).astype(BF)
            self.near[k, other] = total[other].astype(BF)
            self.send(self.near.at[k], self.last_in.at[k], 2 + k, d)

    def third(self):
        total = self.term(0)
        for k in (0, 1):
            wait_arrival(self.last_in.at[k], self.recv_sem.at[2 + k])
            total += self.last_in[k].astype(F32)
        for copy in self.sent:
            copy.wait_send()
        return total


def ff_kernel(
    set_ref, own_hbm, cot_hbm, gate_hbm, up_hbm, down_hbm, a_wide, a_down, b_wide, b_ff,
    grad_out, down_out, cols_out, wide_out,
    cols_ref, wide_ref, x_ref, cot_ref, gate_w, up_w, down_w, b_cols, a_cols, hidden_ref, grad_gate, grad_up,
    grad_hidden, own_ref, terms, pair, total_ref, down_sum, a_ff, b_out, wide_sets, down_sets, out_sets,
    ff_sets, sems, out_sems, pair_send, pair_recv, *scratch,
):
    y, z, x, blk, uly = place()
    core = uly % 2
    scratch = list(scratch)

    def take(count):
        got = scratch[:count]
        del scratch[:count]
        return got

    first = (35 * uly) // 2 * 128 + y * FF_COLS
    columns = pl.ds(pl.multiple_of(first, 128), FF_COLS)
    pairs = (
        (own_hbm, own_ref), (down_hbm, down_w), (cot_hbm, cot_ref), (gate_hbm, gate_w), (up_hbm, up_w),
        (a_wide.at[pl.ds(4, 2)], wide_sets), (a_down.at[:, :, columns], down_sets), (b_wide.at[2], out_sets),
        (b_ff.at[:, :, :, columns], ff_sets),
    )
    copies = [pltpu.make_async_copy(src, dst, sems.at[n]) for n, (src, dst) in enumerate(pairs)]
    for copy in copies[:1] + copies[5:] + copies[1:5]:
        copy.start()
    at = lax.broadcasted_iota(jnp.int32, (16, FF_COLS), 1) + (y * FF_COLS - 64 * core)
    inside = jnp.logical_and(at >= 0, at < FF // 4)

    def keep(v):
        return jnp.where(inside, v.astype(F32), 0.0).astype(BF)

    def prepare():
        for copy in copies[5:]:
            copy.wait()
        for s in (0, 1):
            number = set_ref[s]
            a_cols[s] = keep(choose(number, lambda c: down_sets[c]))
            b_out[s] = choose(number, lambda c: out_sets[c])
            for n in (0, 1):
                b_cols[s, n] = keep(choose(number, lambda c: ff_sets[n, c]))
                a_ff[s, 16 * n : 16 * n + 16] = choose(number, lambda c: wide_sets[n, c])
        cols_ref[...] = jnp.zeros_like(cols_ref)

    sibling = uly_others()[1]
    greet([sibling, (blk_of(1 - y, z, x), uly), (blk_of(1 - y, z, x), (uly + 2) % 4)], prepare)
    here = pl.ds(pl.multiple_of(y * FF_COLS, 128), FF_COLS)
    copies[0].wait()
    spread = Spread(own_ref, x_ref, *take(3))
    spread.start()

    def flat(ref, s):
        return ref[s].reshape(4 * CHUNK, D)

    order = (1 - core, core)
    copies[1].wait()
    copies[2].wait()
    latent_cots = []
    for k, s in enumerate(order):
        cot = flat(cot_ref, s)
        latent_cots.append(dot_nt(cot, b_out[s]))
        grad_hidden[k] = dot(cot, down_w[...]) + dot(latent_cots[k].astype(BF), a_cols[s])
        (spread.second, spread.third)[k]()
    copies[3].wait()
    copies[4].wait()
    spread.last()

    def pair_copy(n, d):
        at = (ring_at() + d) % 4
        return remote(
            terms.at[n, 0, at], pair.at[n, at], pair_send.at[n, d], pair_recv.at[n, d], sibling
        )

    def term(n, d):
        at = (ring_at() + d) % 4
        wait_arrival(pair.at[n, at], pair_recv.at[n, d])
        return terms[n, 1, at].astype(F32) + pair[n, at].astype(F32)

    ring = RingSum(lambda d: term(0, d), take(RingSum.scratches))
    for k, s in enumerate(order):
        rows = flat(x_ref, s)
        latent = dot_nt(rows, a_ff[s])
        low = latent.astype(BF)
        gate = dot(rows, gate_w[...]) + dot(low[:, :16], b_cols[s, 0])
        sigmoid = jax.nn.sigmoid(gate)
        silu = gate * sigmoid
        grad_up[...] = (grad_hidden[k] * silu).astype(BF)
        slope = grad_hidden[k] * (sigmoid * (1.0 + gate * (1.0 - sigmoid)))
        up = dot(rows, up_w[...]) + dot(low[:, 16:], b_cols[s, 1])
        grad_gate[...] = (slope * up).astype(BF)
        hidden_ref[...] = (silu * up).astype(BF)
        back_gate = dot_nt(grad_gate[...], b_cols[s, 0])
        back_up = dot_nt(grad_up[...], b_cols[s, 1])
        grads = (
            dot_nt(grad_gate[...], gate_w[...])
            + dot_nt(grad_up[...], up_w[...])
            + dot(back_gate.astype(BF), a_ff[s, :16])
            + dot(back_up.astype(BF), a_ff[s, 16:])
        )
        terms[0, k] = grads.astype(BF).reshape(4, CHUNK, D)
        if k == 0:
            for d in (2, 1, 3, 0):
                pair_copy(0, d).start()
        else:
            ring.first()
        latent_down = dot_nt(hidden_ref[...], a_cols[s])
        down = dot_nt(hidden_ref[...], down_w[...]) + dot(latent_down.astype(BF), b_out[s])
        terms[1, k] = down.astype(BF).reshape(4, CHUNK, D)
        if k == 0:
            for d in (2, 1, 3, 0):
                pair_copy(1, d).start()
        else:
            ring.second()

        def put(ref, n, value, at=slice(None)):
            ref[pl.ds(pl.multiple_of((2 * n + s) * 16, 16), 16), at] = value.astype(BF)

        def turned(value):
            return value.T.astype(BF)

        put(cols_ref, 0, dot(turned(latent_cots[k]), hidden_ref[...]), here)
        put(cols_ref, 1, dot(turned(latent[:, :16]), grad_gate[...]), here)
        put(cols_ref, 2, dot(turned(latent[:, 16:]), grad_up[...]), here)
        put(wide_ref, 0, dot(turned(back_gate), rows))
        put(wide_ref, 1, dot(turned(back_up), rows))
        put(wide_ref, 2, dot(turned(latent_down), flat(cot_ref, s)))
    outs = [
        pltpu.make_async_copy(src, dst, out_sems.at[n])
        for n, (src, dst) in enumerate(
            ((cols_ref, cols_out), (wide_ref, wide_out), (down_sum, down_out), (total_ref, grad_out))
        )
    ]
    outs[0].start()
    outs[1].start()
    for d in range(4):
        down_sum[(ring_at() + d) % 4] = term(1, d).astype(BF)
    outs[2].start()
    total_ref[...] = ring.third()
    outs[3].start()
    for n in (0, 1):
        for d in range(4):
            pair_copy(n, d).wait_send()
    for copy in outs:
        copy.wait()


def feed_forward(*args):
    dma = pltpu.SemaphoreType.DMA
    weight = pltpu.VMEM((D, FF_COLS), BF)
    rows = pltpu.VMEM((4 * CHUNK, FF_COLS), BF)
    pieces = (4, CHUNK, D)
    return pl.pallas_call(
        ff_kernel,
        out_shape=(
            HELD((CHUNK, D), F32),
            HELD(pieces, BF),
            HELD((96, PADDED), BF),
            HELD((96, D), BF),
        ),
        in_specs=[pl.BlockSpec(memory_space=pltpu.SMEM)] + [ANY] * 9,
        out_specs=(ANY,) * 4,
        scratch_shapes=[
            pltpu.VMEM((96, PADDED), BF), pltpu.VMEM((96, D), BF),
            pltpu.VMEM((2,) + pieces, BF), pltpu.VMEM((2,) + pieces, BF),
            weight, weight, weight,
            pltpu.VMEM((2, 2, 16, FF_COLS), BF), pltpu.VMEM((2, 16, FF_COLS), BF),
            rows, rows, rows,
            pltpu.VMEM((2, 4 * CHUNK, FF_COLS), F32),
            pltpu.VMEM((CHUNK, D), BF),
            pltpu.VMEM((2, 2) + pieces, BF), pltpu.VMEM((2,) + pieces, BF),
            pltpu.VMEM((CHUNK, D), F32), pltpu.VMEM(pieces, BF),
            pltpu.VMEM((2, 32, D), BF), pltpu.VMEM((2, 16, D), BF),
            pltpu.VMEM((2, SETS, 16, D), BF), pltpu.VMEM((SETS, 16, FF_COLS), BF),
            pltpu.VMEM((SETS, 16, D), BF), pltpu.VMEM((2, SETS, 16, FF_COLS), BF),
            dma((9,)), dma((4,)), dma((2, 4)), dma((2, 4)),
        ]
        + SPREAD_SEMS
        + RingSum.scratch(),
        compiler_params=pltpu.CompilerParams(
            collective_id=4, has_side_effects=True, vmem_limit_bytes=62 * 2**20
        ),
        name="feed_forward",
    )(*args)


def backward_blocks(slot, first, last, turned_ref, rows_ref, dot_ref, kv_ref, limit_ref, lse_ref, dkv_ref, acc_ref):
    limit = limit_ref[slot, 0:1, :]
    lse = lse_ref[slot, 0:1, :]
    row_dot = dot_ref[slot, 0:1, :]

    def step(n, carry):
        keys, values = key_block(kv_ref, n, KEYS_BACK)
        scores = jnp.where(key_places(n, KEYS_BACK) <= limit, dot(keys, turned_ref[0, slot]), -1e30)
        probs = jnp.exp2(scores - lse)
        grad_probs = dot(values, turned_ref[1, slot])
        grad_scores = (probs * (grad_probs - row_dot)).astype(BF)
        acc_ref[slot] += dot(keys.T, grad_scores)
        at = pl.ds(pl.multiple_of(n * KEYS_BACK, KEYS_BACK), KEYS_BACK)
        dkv_ref[at, :HEAD] += dot(grad_scores, rows_ref[0, slot])
        dkv_ref[at, HEAD:] += dot(probs.astype(BF), rows_ref[1, slot])
        return carry

    lax.fori_loop(first, last, step, 0)


class Reduce:
    @staticmethod
    def scratch(shape):
        return [
            pltpu.VMEM((2, 3, 2, 4) + shape, BF),
            pltpu.VMEM((2, 3, 2) + shape, BF),
            pltpu.VMEM((2,) + shape, BF),
            pltpu.VMEM((2, 4, 2) + shape, BF),
            pltpu.VMEM((2, 2) + shape, BF),
            pltpu.SemaphoreType.DMA((2, 10)),
            pltpu.SemaphoreType.DMA((2, 10)),
        ]

    scratches = 7

    def __init__(self, part, scratch):
        self.part = part
        self.buf_q, self.buf_p, self.buf_y, self.sum_p, self.sum_y, self.send_sem, self.recv_sem = scratch
        self.y, self.z, self.x, self.blk, self.uly = place()
        self.pq = ((self.x, self.z), (self.z, self.x))
        self.flying = []

    def send(self, src, dst, half, n, y, p, q):
        target = blk_of(y, q, p) if half == 0 else blk_of(y, p, q)
        copy = remote(
            src, dst, self.send_sem.at[half, n], self.recv_sem.at[half, n], (target, self.uly)
        )
        copy.start()
        self.flying.append(copy)

    def land(self):
        for copy in self.flying:
            copy.wait()
        self.flying = []

    def first(self):
        for d in (2, 1, 3):
            for half in (0, 1):
                p, q = self.pq[half]
                to = (q + d) % 4
                for y in (0, 1):
                    src = self.part.at[0, y, to] if half == 0 else self.part.at[1, y, :, to]
                    self.send(
                        src, self.buf_q.at[half, d - 1, y], half, (d - 1) * 2 + y, self.y, p, to
                    )

    def second(self):
        self.land()
        for d in (2, 1, 3, 0):
            for half in (0, 1):
                p, q = self.pq[half]
                to = (p + d) % 4
                for y in (0, 1):
                    own = self.part[0, y, q, to] if half == 0 else self.part[1, y, to, q]
                    total = own.astype(F32)
                    for n in range(3):
                        total += self.buf_q[half, n, y, to].astype(F32)
                    self.sum_p[half, d, y] = total.astype(BF)
                if d > 0:
                    self.send(
                        self.sum_p.at[half, d], self.buf_p.at[half, d - 1], half, 5 + d, self.y, to, q
                    )

    def third(self):
        self.land()
        for k in (1, 0):
            for half in (0, 1):
                p, q = self.pq[half]
                y = self.y if k == 0 else 1 - self.y
                total = self.sum_p[half, 0, y].astype(F32)
                for n in range(3):
                    total += self.buf_p[half, n, y].astype(F32)
                self.sum_y[half, k] = total.astype(BF)
                if k == 1:
                    self.send(self.sum_y.at[half, 1], self.buf_y.at[half], half, 9, 1 - self.y, p, q)

    def fourth(self):
        self.land()
        return [self.sum_y[half, 0].astype(F32) + self.buf_y[half].astype(F32) for half in (0, 1)]


class Shed:
    @staticmethod
    def scratch(shape):
        return [
            pltpu.VMEM((2, 4) + shape, BF),
            pltpu.VMEM((2, 4) + shape, BF),
            pltpu.VMEM((2, 2, 4) + shape, BF),
            pltpu.VMEM((4, 2) + shape, BF),
            pltpu.VMEM((3, 2) + shape, BF),
            pltpu.VMEM((2,) + shape, BF),
            pltpu.VMEM(shape, BF),
            pltpu.SemaphoreType.DMA((10,)),
            pltpu.SemaphoreType.DMA((10,)),
        ]

    scratches = 9

    def __init__(self, part, half, rows, order, scratch):
        self.part, self.half, self.rows, self.order = part, half, rows, order
        (
            self.buf_far, self.sum_mid, self.buf_in, self.sum_p, self.buf_p, self.sum_y, self.buf_y,
            self.send_sem, self.recv_sem,
        ) = scratch
        self.y, self.z, self.x, self.blk, self.uly = place()
        self.p, self.q = (self.x, self.z) if order == 0 else (self.z, self.x)
        self.flying = []

    def line(self, y, q):
        rows = pl.ds(*self.rows)
        if self.order == 0:
            return self.part.at[self.half, y, q, :, rows]
        return self.part.at[self.half, y, :, q, rows]

    def value(self, y, q, p):
        start, size = self.rows
        z, x = (q, p) if self.order == 0 else (p, q)
        return self.part[self.half, y, z, x, start : start + size].astype(F32)

    def send(self, src, dst, n, y, p, q):
        target = blk_of(y, q, p) if self.order == 0 else blk_of(y, p, q)
        copy = remote(src, dst, self.send_sem.at[n], self.recv_sem.at[n], (target, self.uly))
        copy.start()
        self.flying.append(copy)

    def land(self):
        for copy in self.flying:
            copy.wait()
        self.flying = []

    def first(self):
        for y, d in ((0, 1), (1, 3)):
            to = (self.q + d) % 4
            self.send(self.line(y, (self.q + 2) % 4), self.buf_far.at[y], y, self.y, self.p, to)
        for y, d in ((1, 1), (0, 3)):
            to = (self.q + d) % 4
            self.send(self.line(y, to), self.buf_in.at[d // 2, y], 2 + d // 2, self.y, self.p, to)

    def second(self):
        direct = self.flying[2:]
        self.flying = self.flying[:2]
        self.land()
        for y, d in ((0, 1), (1, 3)):
            to = (self.q + d) % 4
            for p in range(4):
                total = self.value(y, to, p) + self.buf_far[y, p].astype(F32)
                self.sum_mid[y, p] = total.astype(BF)
            self.send(self.sum_mid.at[y], self.buf_in.at[d // 2, y], 4 + y, self.y, self.p, to)
        self.flying += direct

    def third(self):
        self.land()
        for d in (2, 1, 3, 0):
            to = (self.p + d) % 4
            for y in (0, 1):
                total = self.value(y, self.q, to)
                for n in (0, 1):
                    total += self.buf_in[n, y, to].astype(F32)
                self.sum_p[d, y] = total.astype(BF)
            if d > 0:
                self.send(self.sum_p.at[d], self.buf_p.at[d - 1], 5 + d, self.y, to, self.q)

    def fourth(self):
        self.land()
        for k in (1, 0):
            y = self.y if k == 0 else 1 - self.y
            total = self.sum_p[0, y].astype(F32)
            for n in range(3):
                total += self.buf_p[n, y].astype(F32)
            self.sum_y[k] = total.astype(BF)
            if k == 1:
                self.send(self.sum_y.at[1], self.buf_y, 9, 1 - self.y, self.p, self.q)

    def last(self):
        self.land()
        return self.sum_y[0].astype(F32) + self.buf_y[...].astype(F32)


def reduce_others():
    y, z, x, blk, uly = place()
    return (
        [(blk_of(1 - y, z, x), uly)]
        + [(blk_of(y, z, (x + d) % 4), uly) for d in (1, 2, 3)]
        + [(blk_of(y, (z + d) % 4, x), uly) for d in (1, 2, 3)]
    )


UNIT = (16, 128)


class Total:
    @staticmethod
    def scratch(kept, summed):
        shape = (kept + summed,) + UNIT
        return (
            [pltpu.VMEM((2, 2, 4, 4) + shape, BF)]
            + Reduce.scratch(shape)
            + [
                pltpu.VMEM((2,) + shape, BF),
                pltpu.VMEM((3, 2) + shape, BF),
                pltpu.VMEM((2, 4 * kept + summed) + UNIT, BF),
                pltpu.SemaphoreType.DMA((3,)),
                pltpu.SemaphoreType.DMA((3,)),
                pltpu.SemaphoreType.DMA((31,)),
                pltpu.SemaphoreType.DMA((31,)),
                pltpu.SemaphoreType.DMA,
                pltpu.SemaphoreType.DMA,
                pltpu.SemaphoreType.DMA,
            ]
        )

    scratches = 18

    @staticmethod
    def shape(kept, summed):
        return HELD((2, 2, 4, 4, 4 * kept + summed) + UNIT, BF)

    def __init__(self, kept, summed, all_ref, scratch):
        self.kept, self.summed, self.all_ref = kept, summed, all_ref
        self.part = scratch[0]
        self.reduce = Reduce(self.part, scratch[1:8])
        self.own, self.buf, self.full, self.send_sem, self.recv_sem = scratch[8:13]
        self.all_send, self.all_recv, self.local_sem, self.pair_send, self.pair_recv = scratch[13:18]
        self.y, self.z, self.x, self.blk, self.uly = place()
        self.core = self.uly % 2
        self.flying = []

    def pack(self, values, first, per, at):
        for n, value in enumerate(values, first):
            item = n // per
            self.part[item // 32, item // 16 % 2, item // 4 % 4, item % 4, at + n % per] = value.astype(BF)

    def pack_kept(self, values, first=0):
        self.pack(values, first, self.kept, 0)

    def pack_summed(self, values, first=0):
        self.pack(values, first, self.summed, self.kept)

    def clear(self, kept, summed):
        nothing = jnp.zeros(UNIT, BF)
        self.pack_kept([nothing] * (64 * self.kept - kept), kept)
        self.pack_summed([nothing] * (64 * self.summed - summed), summed)

    def across(self):
        for half, total in enumerate(self.reduce.fourth()):
            self.own[half] = total.astype(BF)
        self.copies = []
        for n, other in enumerate(uly_others()):
            copy = remote(self.own, self.buf.at[n], self.send_sem.at[n], self.recv_sem.at[n], other)
            copy.start()
            self.copies.append(copy)

    def send(self, src, dst, n, y, z, x):
        copy = remote(src, dst, self.all_send.at[n], self.all_recv.at[n], (blk_of(y, z, x), self.uly))
        copy.start()
        self.flying.append(copy)

    def item(self, y, d=0, e=0):
        dz, dx = self.core * d + (1 - self.core) * e, self.core * e + (1 - self.core) * d
        return self.all_ref.at[self.core, y, (self.z + dz) % 4, (self.x + dx) % 4]

    def along(self, y, src, n, d, e):
        dz, dx = self.core * d + (1 - self.core) * e, self.core * e + (1 - self.core) * d
        self.send(src[0], src[1], n, self.y, (self.z + dz) % 4, (self.x + dx) % 4)

    def along_first(self, y, src, first):
        for d in (1, 2, 3):
            self.along(y, (src, self.item(y)), first + d, d, 0)

    def join(self):
        for copy in self.copies:
            copy.wait()
        kept = self.kept
        terms = [self.own] + [self.buf.at[n] for n in range(3)]
        who = [self.uly] + [other[1] for other in uly_others()]
        for half in (0, 1):
            for term, uly in zip(terms, who):
                self.full[half, pl.ds(uly * kept, kept)] = term[half, :kept]
            if self.summed:
                self.full[half, 4 * kept :] = sum(
                    term[half, kept:].astype(F32) for term in terms
                ).astype(BF)
        own = self.full.at[self.core]
        self.send(own, self.item(self.y), 0, 1 - self.y, self.z, self.x)
        self.along_first(self.y, own, 0)
        self.local = pltpu.make_async_copy(own, self.item(self.y), self.local_sem)
        self.local.start()

    def onward(self):
        other = self.item(1 - self.y)
        wait_arrival(other, self.all_recv.at[0])
        self.along_first(1 - self.y, other, 3)

    def spread(self):
        self.local.wait()
        for k, y in enumerate((self.y, 1 - self.y)):
            for d in range(4):
                if d > 0:
                    wait_arrival(self.item(y, 4 - d), self.all_recv.at[3 * k + d])
                for e in (1, 2, 3):
                    ref = self.item(y, (4 - d) % 4)
                    self.along(y, (ref, ref), 7 + k * 12 + d * 3 + e - 1, 0, e)

    def hand(self):
        for k, y in enumerate((self.y, 1 - self.y)):
            for d in range(4):
                for e in (1, 2, 3):
                    wait_arrival(
                        self.item(y, (4 - d) % 4, 4 - e), self.all_recv.at[7 + k * 12 + d * 3 + e - 1]
                    )
        self.pair(self.core).start()

    def pair(self, core):
        return remote(
            self.all_ref.at[core], self.all_ref.at[core], self.pair_send, self.pair_recv, uly_others()[1]
        )

    def end(self):
        for copy in self.flying:
            copy.wait_send()
        self.pair(self.core).wait_send()
        wait_arrival(self.all_ref.at[1 - self.core], self.pair_recv)

    def steps(self):
        return [
            self.reduce.first, self.reduce.second, self.reduce.third, self.across, self.join,
            self.onward, self.spread, self.hand, self.end,
        ]


def units(value):
    rows, columns = value.shape
    return [
        value[n * 16 : (n + 1) * 16, t * 128 : (t + 1) * 128]
        for n in range(rows // 16) for t in range(columns // 128)
    ]


FF_KEPT, FF_SUMMED, QKV_KEPT = 2, 2, 1
COL_TILES = PADDED // 128
D_TILES = D // 128
DKV_ROWS = CHUNK // 2
DKV_STREAMS = 2


def backward_kernel(
    gains_hbm, total_hbm, down_hbm, cols_hbm, ff_hbm, resid_hbm, cot_hbm, ao_hbm, mixed_hbm, wo_hbm, kv_hbm, q_hbm, limit_hbm, lse_hbm,
    wq_hbm, rows_hbm, normed_hbm, b_qkv_hbm, cos_hbm, sin_hbm, a_hbm, bo_hbm,
    result_ref, input_grad_ref, ff_all, qkv_all,
    gains_ref, total_ref, down_ref, cols_ref, ff_ref, resid_ref, cot_ref, ao_ref, mixed_ref, wo_ref, kv_ref, q_ref, limit_ref,
    lse_ref, wq_ref, rows_ref, normed_ref, b_qkv_ref, cos_ref, sin_ref, a_ref, bo_ref, dkv_ref, acc_ref, part, dq_ref, grad_ref, grad_attn, grad_resid, grad_qkv,
    cross_out, cross_in, home_out, home_in, turned_ref, by_rows_ref, dot_ref, copy_sem, cross_sem, home_send,
    home_recv, *scratch,
):
    y, z, x, blk, uly = place()
    core, h = uly % 2, uly // 2
    scratch = list(scratch)

    def take(count):
        got = scratch[:count]
        del scratch[:count]
        return got

    chunk = 2 * blk + h
    upper = chunk // 32
    home = (1 - h) * blk + h * (31 - blk)
    home_from = [(home, upper * 2 + s) for s in (0, 1)]
    lower = low_chunk(blk)
    own_chunk = (1 - h) * lower + h * (63 - lower)
    home_to = [(own_chunk // 2, (own_chunk % 2) * 2 + half) for half in (0, 1)]
    copies = [
        pltpu.make_async_copy(src, dst, copy_sem.at[n])
        for n, (src, dst) in enumerate(
            (
                (total_hbm, total_ref), (resid_hbm, resid_ref), (cot_hbm, cot_ref), (gains_hbm, gains_ref),
                (cols_hbm, cols_ref), (ff_hbm, ff_ref), (down_hbm, down_ref), (ao_hbm, ao_ref), (mixed_hbm, mixed_ref),
                (wo_hbm, wo_ref), (bo_hbm, bo_ref), (kv_hbm, kv_ref),
                (q_hbm, q_ref), (limit_hbm, limit_ref), (lse_hbm, lse_ref), (wq_hbm, wq_ref),
                (rows_hbm, rows_ref), (normed_hbm, normed_ref), (b_qkv_hbm, b_qkv_ref),
                (cos_hbm, cos_ref), (sin_hbm, sin_ref), (a_hbm, a_ref),
            )
        )
    ]
    for copy in copies:
        copy.start()
    greet(
        reduce_others() + uly_others() + [(blk_of(1 - y, z, x), (uly + 2) % 4)] + home_from + home_to
    )
    collect_out = RingSum(
        lambda d: down_ref[(ring_at() + d) % 4].astype(F32), take(RingSum.scratches)
    )
    low, high = (
        [
            Shed(part, half, (n * DKV_ROWS, DKV_ROWS), n, take(Shed.scratches))
            for n in range(DKV_STREAMS)
        ]
        for half in (0, 1)
    )
    ff_total = Total(FF_KEPT, FF_SUMMED, ff_all, take(Total.scratches))
    qkv_total = Total(QKV_KEPT, 0, qkv_all, take(Total.scratches))
    deliver = Deliver()

    def send_home(n, value):
        home_out[n] = value.astype(BF)
        for half in (0, 1):
            deliver.send(
                home_out.at[n, pl.ds(half * 64, 64)], home_in.at[n, core],
                home_send.at[n, half], home_recv.at[n, core], home_to[half],
            )

    def arrived_home(n):
        for s in (0, 1):
            wait_arrival(home_in.at[n, s], home_recv.at[n, s])
        return home_in[n].astype(F32)

    def ready(first, last):
        for copy in copies[first:last]:
            copy.wait()

    ready(0, 4)
    residual = resid_ref[...]
    value = cot_ref[...].astype(F32) + norm_back(
        residual, norm_scale(residual), gain(gains_ref, D_TILES), total_ref[...]
    )
    grad_resid[...] = value
    own_rows = pl.ds(pl.multiple_of(h * CHUNK, CHUNK), CHUNK)
    other_rows = pl.ds(pl.multiple_of((1 - h) * CHUNK, CHUNK), CHUNK)
    grad_attn[own_rows, :] = value.astype(BF)
    partner = uly_others()[0]
    cross = remote(
        grad_attn.at[own_rows], grad_attn.at[own_rows], cross_sem.at[0], cross_sem.at[1], partner
    )
    cross.start()
    ready(4, 11)
    ff_total.pack_kept(units(cols_ref))
    ff_total.pack_summed(units(ff_ref))
    ff_total.clear(6 * COL_TILES, 6 * D_TILES)
    steps = ff_total.steps()

    def beside(*more):
        for step in more:
            step()
        if steps:
            steps.pop(0)()

    beside()
    at_o = 3 * D_TILES + D_TILES // 2 + 2
    qkv_total.clear(at_o + D_TILES // 2 + D_TILES, 0)
    dkv_ref[...] = jnp.zeros_like(dkv_ref)
    acc_ref[...] = jnp.zeros_like(acc_ref)
    latent_o = dot_nt(ao_ref[...], mixed_ref[...]).astype(BF)
    cross.wait_send()
    wait_arrival(grad_attn.at[other_rows], cross_sem.at[1])
    back_o = dot_nt(grad_attn[...], bo_ref[...]).astype(BF)
    grad_ref[...] = (dot_nt(grad_attn[...], wo_ref[...]) + dot(back_o, ao_ref[...])).astype(BF)
    back_o = dot_nt(bo_ref[...], grad_attn[...]).astype(BF)
    qkv_total.pack_kept(
        units(dot(back_o, mixed_ref[...])) + units(dot(latent_o, grad_attn[...])), at_o
    )
    beside()

    ready(11, 15)
    def pack(half):
        def one(n, carry):
            chunk = low_chunk(n) if half == 0 else 63 - low_chunk(n)
            rows = dkv_ref[pl.ds(pl.multiple_of(chunk * CHUNK, CHUNK), CHUNK), :]
            both = jnp.concatenate([rows[:, :HEAD] * LN2, rows[:, HEAD:]], axis=1)
            part[half, n // 16, n // 4 % 4, n % 4] = both.astype(BF)
            return carry

        lax.fori_loop(0, 32, one, 0)

    def shed(streams, name):
        def run():
            for stream in streams:
                getattr(stream, name)()

        return run

    args = (turned_ref, by_rows_ref, dot_ref, kv_ref, limit_ref, lse_ref, dkv_ref, acc_ref)
    step = KEYS_BACK // CHUNK
    middle = CHUNKS // 2 // step
    beside()
    for slot in (0, 1):
        for n, ref in enumerate((q_ref, grad_ref)):
            turned_ref[n, slot] = head_columns(ref, slot)
            by_rows_ref[n, slot] = head_rows(ref, slot)
        row_dot = turned_ref[1, slot].astype(F32) * head_columns(mixed_ref, slot).astype(F32)
        dot_ref[slot] = jnp.broadcast_to(jnp.sum(row_dot, axis=0, keepdims=True), (8, ROWS))
    backward_blocks(1, middle, (63 - lower) // step + 1, *args)
    backward_blocks(0, 0, lower // step + 1, *args)
    pack(1)
    beside(shed(high, "first"))
    names = ["second", "third", "fourth"]
    extra = [collect_out.first, collect_out.second]
    for n in range(0, middle, 2):
        backward_blocks(1, n, n + 2, *args)
        more = [shed(high, names.pop(0))] if names else []
        more += [extra.pop(0)] if extra else []
        if n < middle - 2:
            beside(*more)
    pack(0)
    for stream in low:
        stream.first()
    for slot in (0, 1):
        for n in range(GROUP):
            dq_ref[slot * CHUNK : (slot + 1) * CHUNK, n * HEAD : (n + 1) * HEAD] = (
                acc_ref[slot, :, n * CHUNK : (n + 1) * CHUNK].T * HEAD ** (-0.5)
            )
    ready(15, 22)
    a_qkv = a_ref[...].reshape(48, D)
    for stream in low:
        stream.second()
    beside()
    cos_table, sine_table = cos_ref[...], sin_ref[...]

    def turn_back(value, rows=slice(None)):
        return value * cos_table[rows] - pltpu.roll(value, HEAD // 2, 1) * sine_table[rows]

    for n in range(GROUP):
        at = slice(n * HEAD, (n + 1) * HEAD)
        grad_qkv[:, at] = turn_back(dq_ref[:, at]).astype(BF)
    group = GROUP * HEAD

    def key_value(half, streams):
        for n, stream in enumerate(streams):
            rows = slice(half * CHUNK + n * DKV_ROWS, half * CHUNK + (n + 1) * DKV_ROWS)
            value = stream.last()
            grad_qkv[rows, group : group + HEAD] = turn_back(value[:, :HEAD], rows).astype(BF)
            grad_qkv[rows, group + HEAD :] = value[:, HEAD:].astype(BF)

    key_value(1, high)
    for stream in low:
        stream.third()
    send_home(0, resid_ref[...] + collect_out.third())
    latent_qkv = dot_nt(a_qkv, normed_ref[...]).astype(BF)
    for stream in low:
        stream.fourth()
    key_value(0, low)

    def project_back(rows):
        grads = grad_qkv[rows, :]
        lifted = dot(dot_nt(grads, b_qkv_ref[...]).astype(BF), a_qkv)
        return dot_nt(grads[:, :512], wq_ref[0]) + dot_nt(grads[:, 512:], wq_ref[1]) + lifted

    cross_out[...] = project_back(other_rows).astype(BF)
    cross = remote(cross_out, cross_in, cross_sem.at[2], cross_sem.at[3], partner)
    cross.start()
    back_qkv = dot_nt(b_qkv_ref[...], grad_qkv[...]).astype(BF)
    grad_b = dot(latent_qkv, grad_qkv[...])
    qkv_total.pack_kept(
        units(dot(back_qkv, normed_ref[...]))
        + units(grad_b[:16, :group])
        + units(grad_b[16:32, group : group + HEAD])
        + units(grad_b[32:, group + HEAD :])
    )
    last_steps = qkv_total.steps()
    last_steps.pop(0)()
    mine = project_back(own_rows)
    last_steps.pop(0)()
    beside()
    cross.wait()
    mine = mine + cross_in[...].astype(F32)
    tokens = rows_ref[own_rows, :].astype(F32)
    send_home(1, grad_resid[...] + norm_back(tokens, norm_scale(tokens), gain(gains_ref, 0), mine))
    for step in last_steps + steps:
        step()
    result_ref[...] = arrived_home(0).astype(BF)
    input_grad_ref[...] = arrived_home(1).astype(BF)
    deliver.end()


def backward(*args):
    dma = pltpu.SemaphoreType.DMA
    group = GROUP * HEAD
    return pl.pallas_call(
        backward_kernel,
        out_shape=(
            jax.ShapeDtypeStruct((2, CHUNK // 2, D), BF),
            jax.ShapeDtypeStruct((2, CHUNK // 2, D), BF),
            Total.shape(FF_KEPT, FF_SUMMED),
            Total.shape(QKV_KEPT, 0),
        ),
        in_specs=[ANY] * 22,
        out_specs=(IN_VMEM, IN_VMEM, ANY, ANY),
        scratch_shapes=[
            pltpu.VMEM((40, 128), F32),
            pltpu.VMEM((CHUNK, D), F32),
            pltpu.VMEM((4, CHUNK, D), BF),
            pltpu.VMEM((96, PADDED), BF),
            pltpu.VMEM((96, D), BF),
            pltpu.VMEM((CHUNK, D), F32),
            pltpu.VMEM((CHUNK, D), BF),
            pltpu.VMEM((16, group), BF),
            pltpu.VMEM((2 * CHUNK, group), BF),
            pltpu.VMEM((D // 2, D), BF),
            pltpu.VMEM((CHUNKS, CHUNK, 2 * HEAD), BF),
            pltpu.VMEM((2 * CHUNK, group), BF),
            pltpu.VMEM((2, 8, ROWS), jnp.int32),
            pltpu.VMEM((2, 8, ROWS), F32),
            pltpu.VMEM((2, D, 512), BF),
            pltpu.VMEM((2 * CHUNK, D), BF),
            pltpu.VMEM((2 * CHUNK, D), BF),
            pltpu.VMEM((48, 1024), BF),
            pltpu.VMEM((2 * CHUNK, HEAD), F32),
            pltpu.VMEM((2 * CHUNK, HEAD), F32),
            pltpu.VMEM((3, 16, D), BF),
            pltpu.VMEM((16, D), BF),
            pltpu.VMEM((CHUNKS * CHUNK, 2 * HEAD), F32),
            pltpu.VMEM((2, HEAD, ROWS), F32),
            pltpu.VMEM((2, 2, 4, 4, CHUNK, 2 * HEAD), BF),
            pltpu.VMEM((2 * CHUNK, group), F32),
            pltpu.VMEM((2 * CHUNK, group), BF),
            pltpu.VMEM((2 * CHUNK, D), BF),
            pltpu.VMEM((CHUNK, D), F32),
            pltpu.VMEM((2 * CHUNK, 1024), BF),
            pltpu.VMEM((CHUNK, D), BF),
            pltpu.VMEM((CHUNK, D), BF),
            pltpu.VMEM((2, CHUNK, D), BF),
            pltpu.VMEM((2, 2, CHUNK // 2, D), BF),
            pltpu.VMEM((2, 2, HEAD, ROWS), BF),
            pltpu.VMEM((2, 2, ROWS, HEAD), BF),
            pltpu.VMEM((2, 8, ROWS), F32),
            dma((22,)), dma((4,)), dma((2, 2)), dma((2, 2)),
        ]
        + RingSum.scratch()
        + Shed.scratch((DKV_ROWS, 2 * HEAD)) * (2 * DKV_STREAMS)
        + Total.scratch(FF_KEPT, FF_SUMMED)
        + Total.scratch(QKV_KEPT, 0),
        compiler_params=pltpu.CompilerParams(
            collective_id=2, has_side_effects=True, vmem_limit_bytes=60 * 2**20
        ),
        name="backward",
    )(*args)


def fold_kernel(
    set_ref, result_in, grad_in, ff_hbm, qkv_hbm, result_ref, input_grad_ref, a_wide, a_down, b_wide, b_kv, b_ff,
    ff_ref, qkv_ref, sems,
):
    c = pl.program_id(0)
    share = [jnp.where(set_ref[s] == c, 1.0, 0.0) for s in (0, 1)]

    @pl.when(c == 0)
    def _():
        copies = [
            pltpu.make_async_copy(src, dst, sems.at[n])
            for n, (src, dst) in enumerate(((ff_hbm, ff_ref), (qkv_hbm, qkv_ref)))
        ]
        for copy in copies:
            copy.start()
        result_ref[...] = result_in[...]
        input_grad_ref[...] = grad_in[...].astype(F32)
        for copy in copies:
            copy.wait()

    def kept(ref, per, n, u):
        item = n // per
        return ref[item // 32, item // 16 % 2, item // 4 % 4, item % 4, u * per + n % per].astype(F32)

    def ff_kept(n, u):
        return kept(ff_ref, FF_KEPT, n, u)

    def qkv_kept(n, u):
        return kept(qkv_ref, QKV_KEPT, n, u)

    def summed(n):
        item = n // FF_SUMMED
        return ff_ref[
            item // 32, item // 16 % 2, item // 4 % 4, item % 4, 4 * FF_KEPT + n % FF_SUMMED
        ].astype(F32)

    def put(ref, at, tile, value):
        ref[at + (slice(None), slice(tile * 128, (tile + 1) * 128))] = (
            share[0] * value(0) + share[1] * value(1)
        )

    for n in range(3):
        for t in range(D_TILES):
            put(a_wide, (n, 0), t, lambda s: qkv_kept(n * D_TILES + t, s) + qkv_kept(n * D_TILES + t, 2 + s))
    half = D_TILES // 2
    at_o = 3 * D_TILES + half + 2
    for t in range(D_TILES):
        h, part = t // half, t % half
        put(a_wide, (3, 0), t, lambda s: qkv_kept(at_o + part, 2 * h + s))
        put(b_wide, (0, 0), t, lambda s: qkv_kept(3 * D_TILES + part, 2 * h + s))
        put(
            b_wide, (1, 0), t,
            lambda s: qkv_kept(at_o + half + t, s) + qkv_kept(at_o + half + t, 2 + s),
        )
        for n, (ref, at) in enumerate(((a_wide, (4, 0)), (a_wide, (5, 0)), (b_wide, (2, 0)))):
            put(ref, at, t, lambda s: summed((2 * n + s) * D_TILES + t))
    for n in (0, 1):
        for h in (0, 1):
            put(b_kv, (n, 0), h, lambda s: qkv_kept(3 * D_TILES + half + n, 2 * h + s))
    for n, (ref, at) in enumerate(((a_down, (0,)), (b_ff, (0, 0)), (b_ff, (1, 0)))):
        for t in range(FF // 128):
            where = [
                (u, t - start) for u, start in enumerate((0, 17, 35, 52)) if 0 <= t - start < COL_TILES
            ]
            put(
                ref, at, t,
                lambda s: sum(ff_kept((2 * n + s) * COL_TILES + tile, u) for u, tile in where),
            )


def fold(set_index, result, input_grad, ff_all, qkv_all):
    rows = pl.BlockSpec(result.shape, lambda c: (0, 0, 0))

    def by_set(lead, columns):
        shape = lead + (1, 16, columns)
        return pl.BlockSpec(shape, lambda c: (0,) * len(lead) + (c, 0, 0))

    def out(lead, columns):
        return jax.ShapeDtypeStruct(lead + (SETS, 16, columns), F32)

    outs = (((6,), D), ((), FF), ((3,), D), ((2,), 2 * HEAD), ((2,), FF))
    return pl.pallas_call(
        fold_kernel,
        grid=(SETS,),
        out_shape=(
            jax.ShapeDtypeStruct(result.shape, BF),
            jax.ShapeDtypeStruct(result.shape, F32),
        )
        + tuple(out(*o) for o in outs),
        in_specs=[pl.BlockSpec(memory_space=pltpu.SMEM), rows, rows, ANY, ANY],
        out_specs=(rows, rows) + tuple(by_set(*o) for o in outs),
        scratch_shapes=[
            pltpu.VMEM(ff_all.shape, BF), pltpu.VMEM(qkv_all.shape, BF), pltpu.SemaphoreType.DMA((2,))
        ],
        compiler_params=pltpu.CompilerParams(vmem_limit_bytes=40 * 2**20),
        name="fold",
    )(set_index, result, input_grad, ff_all, qkv_all)


def norm_scale(hidden):
    return lax.rsqrt(jnp.mean(hidden * hidden, axis=-1, keepdims=True) + EPS)


def norm_back(hidden, scaled, gain_vec, upstream):
    normed = hidden * scaled
    weighted = upstream * gain_vec
    return scaled * (weighted - normed * jnp.mean(weighted * normed, axis=-1, keepdims=True))


def held(*arrays):
    return [pltpu.with_memory_space_constraint(v, pltpu.HBM) for v in arrays]


def body(
    tokens, cotangent, lengths, set_index, norm_in, norm_ff, qkv_bias, w_qkv, w_out, w_gate_up, w_down,
    a_wide, a_down, b_wide, b_kv, b_ff,
):
    frequencies = np.float64(THETA) ** (-np.arange(0, HEAD, 2, dtype=np.float64) / HEAD)
    frequencies = jnp.asarray(np.concatenate([frequencies, frequencies])[None].astype(np.float32))
    gains = jnp.concatenate([norm_in, norm_ff, qkv_bias]).reshape(40, 128)
    (
        q, mixed, lse, kv_all, qkv_w, out_w, gate_w, up_w, down_w, rows, normed, residual, grad_out,
        normed_ff, grad_gathered, limit, cos_table, sine_table, b_qkv, ao, a_own, bo,
    ) = forward(
        *held(
            tokens, cotangent, lengths, set_index, w_qkv, w_out, w_gate_up, w_down.T, gains, frequencies,
            a_wide, b_wide, b_kv,
        )
    )
    gate_w, up_w, down_w = (w.reshape(D, FF_COLS) for w in (gate_w, up_w, down_w))
    grad_normed_ff, down_sum, cols, ff_wide = feed_forward(
        set_index, normed_ff, grad_gathered, gate_w, up_w, down_w, *held(a_wide, a_down, b_wide, b_ff)
    )
    result, input_grad, ff_all, qkv_all = backward(
        gains,
        grad_normed_ff, down_sum, cols, ff_wide, residual, grad_out, ao, mixed, out_w, kv_all, q, limit, lse,
        qkv_w, rows, normed, b_qkv, cos_table, sine_table, a_own, bo,
    )
    return tuple(fold(set_index, *held(result, input_grad, ff_all, qkv_all)))


def solution(mesh):
    spread = P(None, ("blk", "uly"), None)
    in_specs = (
        spread, spread, P(), P(), P(), P(), P(),
        P(("blk", "uly"), None), P(("blk", "uly"), None), P(None, "blk", "uly"), P("uly", "blk"),
        P(), P(), P(), P(), P(),
    )
    out_specs = (spread, spread, P(), P(), P(), P(), P())
    return jax.shard_map(body, mesh=mesh, in_specs=in_specs, out_specs=out_specs, check_vma=False)
```

profile of v0, /device:TPU:1, one launch (start us, length us, event | category | flops | bytes accessed | tf_op | source)
XLA Modules:
  0.0 355.6 jit_solution(11909166009301916438)
XLA Ops:
  0.6 1.3 maximum_bitcast_fusion.gains_hbm
  2.0 134.6 %forward.1 = (bf16[256,768]{1,0:T(8,128)(2,1)}, bf16[256,768]{1,0:T(8,128)(2,1)}, f32[2,8,768]{2,1,0:T(8,128)}, bf16[64,128,256]{2,1,0:T(8,128)(2,1)}, bf16[2,15...) custom-call(bf16[2,64,1536]{2,1,0:T(8,128)(2,1)} %tokens_ref.1, ...), custom_call_target="tpu_custom_call" | custom-call | tf_op jit(solution)/shard_map/forward/pallas_call | solution.py:806
  136.5 80.8 %feed_forward.1 = (f32[128,1536]{1,0:T(8,128)}, bf16[4,128,1536]{2,1,0:T(8,128)(2,1)}, bf16[96,2304]{1,0:T(8,128)(2,1)}, bf16[96,1536]{1,0:T(8,128)(2,1)}) custom-call(s32[2]{0:T(128)} %set_ref.3, bf16[128,1536]{1,0:T(8,128)(2,1)} %get-tuple-element.37.own_hbm, bf16[2,4,128,1536]{3,2,1,0:T(8,128)(2,1)} %get-tuple-element.38.cot_hbm, ...), custom_call_target="tpu_custom_call" | custom-call | tf_op jit(solution)/shard_map/feed_forward/pallas_call | solution.py:1100
  217.3 0.0 copy-start
  217.3 125.6 %backward.1 = (bf16[2,64,1536]{2,1,0:T(8,128)(2,1)}, bf16[2,64,1536]{2,1,0:T(8,128)(2,1)}, bf16[2,2,4,4,10,16,128]{6,5,4,3,2,1,0:T(8,128)(2,1)}, bf16[2,2,4,4,4,16,128]{6,5,4,3,2,1,0:T(8,128)(2,1)}) custom-call(f32[40,128]{1,0:T(8,128)} %maximum_bitcast_fusion.gains_hbm, f32[128,1536]{1,0:T(8,128)} %get-tuple-element.42.total_hbm, ...), custom_call_target="tpu_custom_call" | custom-call | tf_op jit(solution)/shard_map/backward/pallas_call | solution.py:1729
  342.9 0.0 copy-done
  342.9 12.2 %fold.1 = (bf16[2,64,1536]{2,1,0:T(8,128)(2,1)}, f32[2,64,1536]{2,1,0:T(8,128)}, f32[6,8,16,1536]{3,2,1,0:T(8,128)}, f32[8,16,8960]{2,1,0:T(8,128)}, f32[3,8,16,...) custom-call(s32[2]{0:T(128)S(1)} %copy-done, ...), custom_call_target="tpu_custom_call" | custom-call | tf_op jit(solution)/shard_map/fold/pallas_call | solution.py:1871
Async XLA Ops:
  217.3 125.6 %copy-start = (s32[2]{0:T(128)S(1)}, s32[2]{0:T(128)}, u32[]{:S(2)}) copy-start(s32[2]{0:T(128)} %set_ref.3) | copy-start | bytes 28
where the time goes:
time: 363 us; the launch traced here: 356 us
  Pallas kernels  353 us (97%)
    pallas_call x1, Pallas kernels, forward(): pl.pallas_call(forward_kernel, out_shape=(HELD((2 * CHUNK, group), BF), H...  135 us
    pallas_call x1, Pallas kernels, backward(): pl.pallas_call(backward_kernel, out_shape=(jax.ShapeDtypeStruct((2, CHUNK...  126 us
    pallas_call x1, Pallas kernels, feed_forward(): pl.pallas_call(ff_kernel, out_shape=(HELD((CHUNK, D), F32), HELD(pieces,...  80.8 us
    pallas_call x1, Pallas kernels, fold(): pl.pallas_call(fold_kernel, grid=(SETS,), out_shape=(jax.ShapeDtypeStruct...  12.2 us

commit v1 on v0

--- a/solution.py
+++ b/solution.py
@@ -375,15 +375,19 @@
 
     def fourth(self, e):
         p = (self.p + e) % 4
-        for d in (4 - self.way, self.way):
+        way = self.way if e % 2 == 0 else 4 - self.way
+        for d in (4 - way, way):
             q = (self.q + d) % 4
             self.wait(p, q)
-            if d == 4 - self.way:
-                self.send(p, q, 0, self.way)
+            if d == 4 - way:
+                self.send(p, q, 0, way)
 
     def last(self):
         for e in (0, 1, 3, 2):
             self.wait((self.p + e) % 4, (self.q + 2) % 4)
+        self.end()
+
+    def end(self):
         for copy in self.sent:
             copy.wait_send()
 
@@ -606,6 +610,7 @@
         *take(3),
     )
     rings = own_ff + other_ff
+    whole = [ring for n, ring in enumerate(rings) if n % 3 != 1]
     def tables(slot):
         at = lower if slot == 0 else 63 - lower
         row = lax.broadcasted_iota(jnp.int32, (CHUNK, HEAD), 0) + at * CHUNK
@@ -650,7 +655,7 @@
         y_copies[2 * n].wait_recv()
     for ring in other_ff:
         ring.start()
-    for ring in rings:
+    for ring in whole:
         ring.spread(0)
 
     for n in range(4):
@@ -719,7 +724,7 @@
     cot_spread.start()
     kv.last()
     for e in (1, 3, 2):
-        for ring in rings:
+        for ring in whole:
             ring.spread(e)
     (out_sem,) = take(1)
     copies = []
@@ -753,11 +758,11 @@
     forward_blocks(0, 0, lower // blocks + 1, *args)
     forward_blocks(1, middle, (63 - lower) // blocks + 1, *args)
     end(0)
-    for ring in rings:
+    for ring in whole:
         ring.fourth(0)
     cot_spread.second()
     forward_blocks(1, 0, middle // 2, *args)
-    for ring in rings:
+    for ring in whole:
         ring.fourth(1)
     cot_spread.third()
     forward_blocks(1, middle // 2, middle, *args)
@@ -776,10 +781,10 @@
     cross_out[...] = project(1 - h).astype(BF)
     cross = remote(cross_out, cross_in, cross_sem.at[0], cross_sem.at[1], uly_others()[0])
     cross.start()
-    for ring in rings:
+    for ring in whole:
         ring.fourth(3)
     mine = project(h) + rows_out[pl.ds(pl.multiple_of(h * CHUNK, CHUNK), CHUNK), :].astype(F32)
-    for ring in rings:
+    for ring in whole:
         ring.fourth(2)
     cross.wait()
     residual = mine + cross_in[...].astype(F32)
@@ -788,8 +793,10 @@
     nf_own[...] = (residual * norm_scale(residual) * gain(gains_ref, D_TILES)).astype(BF)
     keep((nf_own, nf_out))
     cot_spread.last()
-    for ring in rings:
+    for ring in whole:
         ring.last()
+    for ring in (own_ff[1], other_ff[1]):
+        ring.end()
     for n in range(3):
         y_copies[2 * n].wait_send()
         y_copies[2 * n + 1].wait()
@@ -965,13 +972,27 @@
     first = (35 * uly) // 2 * 128 + y * FF_COLS
     columns = pl.ds(pl.multiple_of(first, 128), FF_COLS)
     pairs = (
-        (own_hbm, own_ref), (down_hbm, down_w), (cot_hbm, cot_ref), (gate_hbm, gate_w), (up_hbm, up_w),
+        (own_hbm, own_ref), (down_hbm, down_w), (cot_hbm, cot_ref), (gate_hbm, gate_w),
         (a_wide.at[pl.ds(4, 2)], wide_sets), (a_down.at[:, :, columns], down_sets), (b_wide.at[2], out_sets),
         (b_ff.at[:, :, :, columns], ff_sets),
     )
     copies = [pltpu.make_async_copy(src, dst, sems.at[n]) for n, (src, dst) in enumerate(pairs)]
-    for copy in copies[:1] + copies[5:] + copies[1:5]:
+    for copy in copies[:1] + copies[4:] + copies[1:4]:
         copy.start()
+    other_blk = blk_of(1 - y, z, x)
+    up_send, up_recv, up_sem = take(3)
+    rings = [
+        Ring(
+            up_w.at[b], lambda item: up_w.at[item], yy, yy, 1 + 2 * k, up_send.at[k], up_recv.at[k]
+        )
+        for k, (yy, b) in enumerate(((y, blk), (1 - y, other_blk)))
+    ]
+    lines = []
+    for k, ring in enumerate(rings):
+        for d in range(4):
+            item = ring.at(ring.y, (ring.p + d) % 4, ring.q)
+            lines.append(pltpu.make_async_copy(up_hbm.at[item], up_w.at[item], up_sem.at[k, d]))
+            lines[-1].start()
     at = lax.broadcasted_iota(jnp.int32, (16, FF_COLS), 1) + (y * FF_COLS - 64 * core)
     inside = jnp.logical_and(at >= 0, at < FF // 4)
 
@@ -979,7 +1000,7 @@
         return jnp.where(inside, v.astype(F32), 0.0).astype(BF)
 
     def prepare():
-        for copy in copies[5:]:
+        for copy in copies[4:]:
             copy.wait()
         for s in (0, 1):
             number = set_ref[s]
@@ -991,11 +1012,16 @@
         cols_ref[...] = jnp.zeros_like(cols_ref)
 
     sibling = uly_others()[1]
-    greet([sibling, (blk_of(1 - y, z, x), uly), (blk_of(1 - y, z, x), (uly + 2) % 4)], prepare)
+    greet([sibling, (other_blk, (uly + 2) % 4)] + ring_others(), prepare)
     here = pl.ds(pl.multiple_of(y * FF_COLS, 128), FF_COLS)
     copies[0].wait()
     spread = Spread(own_ref, x_ref, *take(3))
     spread.start()
+    for copy in lines:
+        copy.wait()
+    for e in (0, 1, 3, 2):
+        for ring in rings:
+            ring.spread(e)
 
     def flat(ref, s):
         return ref[s].reshape(4 * CHUNK, D)
@@ -1009,8 +1035,12 @@
         latent_cots.append(dot_nt(cot, b_out[s]))
         grad_hidden[k] = dot(cot, down_w[...]) + dot(latent_cots[k].astype(BF), a_cols[s])
         (spread.second, spread.third)[k]()
+        for ring in rings:
+            ring.fourth(k)
     copies[3].wait()
-    copies[4].wait()
+    for e in (3, 2):
+        for ring in rings:
+            ring.fourth(e)
     spread.last()
 
     def pair_copy(n, d):
@@ -1025,6 +1055,10 @@
         return terms[n, 1, at].astype(F32) + pair[n, at].astype(F32)
 
     ring = RingSum(lambda d: term(0, d), take(RingSum.scratches))
+
+    def up_weight():
+        return up_w[...].reshape(D, FF_COLS)
+
     for k, s in enumerate(order):
         rows = flat(x_ref, s)
         latent = dot_nt(rows, a_ff[s])
@@ -1034,14 +1068,17 @@
         silu = gate * sigmoid
         grad_up[...] = (grad_hidden[k] * silu).astype(BF)
         slope = grad_hidden[k] * (sigmoid * (1.0 + gate * (1.0 - sigmoid)))
-        up = dot(rows, up_w[...]) + dot(low[:, 16:], b_cols[s, 1])
+        if k == 0:
+            for up_ring in rings:
+                up_ring.last()
+        up = dot(rows, up_weight()) + dot(low[:, 16:], b_cols[s, 1])
         grad_gate[...] = (slope * up).astype(BF)
         hidden_ref[...] = (silu * up).astype(BF)
         back_gate = dot_nt(grad_gate[...], b_cols[s, 0])
         back_up = dot_nt(grad_up[...], b_cols[s, 1])
         grads = (
             dot_nt(grad_gate[...], gate_w[...])
-            + dot_nt(grad_up[...], up_w[...])
+            + dot_nt(grad_up[...], up_weight())
             + dot(back_gate.astype(BF), a_ff[s, :16])
             + dot(back_up.astype(BF), a_ff[s, 16:])
         )
@@ -1110,7 +1147,7 @@
         scratch_shapes=[
             pltpu.VMEM((96, PADDED), BF), pltpu.VMEM((96, D), BF),
             pltpu.VMEM((2,) + pieces, BF), pltpu.VMEM((2,) + pieces, BF),
-            weight, weight, weight,
+            weight, pltpu.VMEM((32, 48, FF_COLS), BF), weight,
             pltpu.VMEM((2, 2, 16, FF_COLS), BF), pltpu.VMEM((2, 16, FF_COLS), BF),
             rows, rows, rows,
             pltpu.VMEM((2, 4 * CHUNK, FF_COLS), F32),
@@ -1120,7 +1157,8 @@
             pltpu.VMEM((2, 32, D), BF), pltpu.VMEM((2, 16, D), BF),
             pltpu.VMEM((2, SETS, 16, D), BF), pltpu.VMEM((SETS, 16, FF_COLS), BF),
             pltpu.VMEM((SETS, 16, D), BF), pltpu.VMEM((2, SETS, 16, FF_COLS), BF),
-            dma((9,)), dma((4,)), dma((2, 4)), dma((2, 4)),
+            dma((8,)), dma((4,)), dma((2, 4)), dma((2, 4)),
+            dma((2, Ring.sends)), dma((2, 16)), dma((2, 4)),
         ]
         + SPREAD_SEMS
         + RingSum.scratch(),
@@ -1807,6 +1845,19 @@
         for copy in copies:
             copy.wait()
 
+    chosen = jnp.logical_or(set_ref[0] == c, set_ref[1] == c)
+
+    @pl.when(jnp.logical_not(chosen))
+    def _():
+        for ref in (a_wide, a_down, b_wide, b_kv, b_ff):
+            ref[...] = jnp.zeros_like(ref)
+
+    @pl.when(chosen)
+    def _():
+        fold_set(share, ff_ref, qkv_ref, a_wide, a_down, b_wide, b_kv, b_ff)
+
+
+def fold_set(share, ff_ref, qkv_ref, a_wide, a_down, b_wide, b_kv, b_ff):
     def kept(ref, per, n, u):
         item = n // per
         return ref[item // 32, item // 16 % 2, item // 4 % 4, item % 4, u * per + n % per].astype(F32)
@@ -1916,7 +1967,7 @@
             a_wide, b_wide, b_kv,
         )
     )
-    gate_w, up_w, down_w = (w.reshape(D, FF_COLS) for w in (gate_w, up_w, down_w))
+    gate_w, down_w = (w.reshape(D, FF_COLS) for w in (gate_w, down_w))
     grad_normed_ff, down_sum, cols, ff_wide = feed_forward(
         set_index, normed_ff, grad_gathered, gate_w, up_w, down_w, *held(a_wide, a_down, b_wide, b_ff)
     )

time: 363 us -> 357 us (0.983)
  Pallas kernels: 353 us -> 348 us
    pallas_call x1, Pallas kernels: 135 us -> 128 us  [forward(): pl.pallas_call(forward_kernel, out_shape=(HELD((2 * CHUNK, group), BF), H...]
where the time goes in v1:
time: 357 us; the launch traced here: 350 us
  Pallas kernels  348 us (97%)
    pallas_call x1, Pallas kernels, backward(): pl.pallas_call(backward_kernel, out_shape=(jax.ShapeDtypeStruct((2, CHUNK...  129 us
    pallas_call x1, Pallas kernels, forward(): pl.pallas_call(forward_kernel, out_shape=(HELD((2 * CHUNK, group), BF), H...  128 us
    pallas_call x1, Pallas kernels, feed_forward(): pl.pallas_call(ff_kernel, out_shape=(HELD((CHUNK, D), F32), HELD(pieces,...  79.2 us
    pallas_call x1, Pallas kernels, fold(): pl.pallas_call(fold_kernel, grid=(SETS,), out_shape=(jax.ShapeDtypeStruct...  11.6 us

profile of v1, /device:TPU:1, one launch (start us, length us, event | category | flops | bytes accessed | tf_op | source)
XLA Modules:
  0.0 350.1 jit_solution(3531787210360631184)
XLA Ops:
  0.6 1.3 maximum_bitcast_fusion.gains_hbm
  2.0 128.0 %forward.1 = (bf16[256,768]{1,0:T(8,128)(2,1)}, bf16[256,768]{1,0:T(8,128)(2,1)}, f32[2,8,768]{2,1,0:T(8,128)}, bf16[64,128,256]{2,1,0:T(8,128)(2,1)}, bf16[2,15...) custom-call(bf16[2,64,1536]{2,1,0:T(8,128)(2,1)} %tokens_ref.1, ...), custom_call_target="tpu_custom_call" | custom-call | tf_op jit(solution)/shard_map/forward/pallas_call | solution.py:813
  130.0 79.2 %feed_forward.1 = (f32[128,1536]{1,0:T(8,128)}, bf16[4,128,1536]{2,1,0:T(8,128)(2,1)}, bf16[96,2304]{1,0:T(8,128)(2,1)}, bf16[96,1536]{1,0:T(8,128)(2,1)}) custom-call(s32[2]{0:T(128)} %set_ref.3, bf16[128,1536]{1,0:T(8,128)(2,1)} %get-tuple-element.37.own_hbm, bf16[2,4,128,1536]{3,2,1,0:T(8,128)(2,1)} %get-tuple-element.38.cot_hbm, ...), custom_call_target="tpu_custom_call" | custom-call | tf_op jit(solution)/shard_map/feed_forward/pallas_call | solution.py:1137
  209.1 0.0 copy-start
  209.1 129.1 %backward.1 = (bf16[2,64,1536]{2,1,0:T(8,128)(2,1)}, bf16[2,64,1536]{2,1,0:T(8,128)(2,1)}, bf16[2,2,4,4,10,16,128]{6,5,4,3,2,1,0:T(8,128)(2,1)}, bf16[2,2,4,4,4,16,128]{6,5,4,3,2,1,0:T(8,128)(2,1)}) custom-call(f32[40,128]{1,0:T(8,128)} %maximum_bitcast_fusion.gains_hbm, f32[128,1536]{1,0:T(8,128)} %get-tuple-element.42.total_hbm, ...), custom_call_target="tpu_custom_call" | custom-call | tf_op jit(solution)/shard_map/backward/pallas_call | solution.py:1767
  338.3 0.0 copy-done
  338.3 11.6 %fold.1 = (bf16[2,64,1536]{2,1,0:T(8,128)(2,1)}, f32[2,64,1536]{2,1,0:T(8,128)}, f32[6,8,16,1536]{3,2,1,0:T(8,128)}, f32[8,16,8960]{2,1,0:T(8,128)}, f32[3,8,16,...) custom-call(s32[2]{0:T(128)S(1)} %copy-done, ...), custom_call_target="tpu_custom_call" | custom-call | tf_op jit(solution)/shard_map/fold/pallas_call | solution.py:1922
Async XLA Ops:
  209.1 129.1 %copy-start = (s32[2]{0:T(128)S(1)}, s32[2]{0:T(128)}, u32[]{:S(2)}) copy-start(s32[2]{0:T(128)} %set_ref.3) | copy-start | bytes 28

commit v2 on v1

--- a/solution.py
+++ b/solution.py
@@ -1195,18 +1195,16 @@
         return [
             pltpu.VMEM((2, 3, 2, 4) + shape, BF),
             pltpu.VMEM((2, 3, 2) + shape, BF),
-            pltpu.VMEM((2,) + shape, BF),
             pltpu.VMEM((2, 4, 2) + shape, BF),
-            pltpu.VMEM((2, 2) + shape, BF),
-            pltpu.SemaphoreType.DMA((2, 10)),
-            pltpu.SemaphoreType.DMA((2, 10)),
+            pltpu.SemaphoreType.DMA((2, 9)),
+            pltpu.SemaphoreType.DMA((2, 9)),
         ]
 
-    scratches = 7
+    scratches = 5
 
     def __init__(self, part, scratch):
         self.part = part
-        self.buf_q, self.buf_p, self.buf_y, self.sum_p, self.sum_y, self.send_sem, self.recv_sem = scratch
+        self.buf_q, self.buf_p, self.sum_p, self.send_sem, self.recv_sem = scratch
         self.y, self.z, self.x, self.blk, self.uly = place()
         self.pq = ((self.x, self.z), (self.z, self.x))
         self.flying = []
@@ -1254,20 +1252,14 @@
 
     def third(self):
         self.land()
-        for k in (1, 0):
-            for half in (0, 1):
-                p, q = self.pq[half]
-                y = self.y if k == 0 else 1 - self.y
-                total = self.sum_p[half, 0, y].astype(F32)
-                for n in range(3):
-                    total += self.buf_p[half, n, y].astype(F32)
-                self.sum_y[half, k] = total.astype(BF)
-                if k == 1:
-                    self.send(self.sum_y.at[half, 1], self.buf_y.at[half], half, 9, 1 - self.y, p, q)
-
-    def fourth(self):
-        self.land()
-        return [self.sum_y[half, 0].astype(F32) + self.buf_y[half].astype(F32) for half in (0, 1)]
+        return [
+            [
+                self.sum_p[half, 0, y].astype(F32)
+                + sum(self.buf_p[half, n, y].astype(F32) for n in range(3))
+                for y in (0, 1)
+            ]
+            for half in (0, 1)
+        ]
 
 
 class Shed:
@@ -1387,20 +1379,20 @@
             [pltpu.VMEM((2, 2, 4, 4) + shape, BF)]
             + Reduce.scratch(shape)
             + [
-                pltpu.VMEM((2,) + shape, BF),
-                pltpu.VMEM((3, 2) + shape, BF),
+                pltpu.VMEM((2, 2) + shape, BF),
+                pltpu.VMEM((4, 2, 2) + shape, BF),
                 pltpu.VMEM((2, 4 * kept + summed) + UNIT, BF),
-                pltpu.SemaphoreType.DMA((3,)),
-                pltpu.SemaphoreType.DMA((3,)),
-                pltpu.SemaphoreType.DMA((31,)),
-                pltpu.SemaphoreType.DMA((31,)),
+                pltpu.SemaphoreType.DMA((7,)),
+                pltpu.SemaphoreType.DMA((8,)),
+                pltpu.SemaphoreType.DMA((15,)),
+                pltpu.SemaphoreType.DMA((15,)),
                 pltpu.SemaphoreType.DMA,
                 pltpu.SemaphoreType.DMA,
                 pltpu.SemaphoreType.DMA,
             ]
         )
 
-    scratches = 18
+    scratches = 16
 
     @staticmethod
     def shape(kept, summed):
@@ -1409,11 +1401,12 @@
     def __init__(self, kept, summed, all_ref, scratch):
         self.kept, self.summed, self.all_ref = kept, summed, all_ref
         self.part = scratch[0]
-        self.reduce = Reduce(self.part, scratch[1:8])
-        self.own, self.buf, self.full, self.send_sem, self.recv_sem = scratch[8:13]
-        self.all_send, self.all_recv, self.local_sem, self.pair_send, self.pair_recv = scratch[13:18]
+        self.reduce = Reduce(self.part, scratch[1:6])
+        self.own, self.buf, self.full, self.send_sem, self.recv_sem = scratch[6:11]
+        self.all_send, self.all_recv, self.local_sem, self.pair_send, self.pair_recv = scratch[11:16]
         self.y, self.z, self.x, self.blk, self.uly = place()
         self.core = self.uly % 2
+        self.w = ring_at()
         self.flying = []
 
     def pack(self, values, first, per, at):
@@ -1432,73 +1425,78 @@
         self.pack_kept([nothing] * (64 * self.kept - kept), kept)
         self.pack_summed([nothing] * (64 * self.summed - summed), summed)
 
+    def others(self):
+        return [
+            ((self.w + d) % 4, self.core if c == 0 else 1 - self.core)
+            for d in range(4) for c in (0, 1) if (d, c) != (0, 0)
+        ]
+
     def across(self):
-        for half, total in enumerate(self.reduce.fourth()):
-            self.own[half] = total.astype(BF)
+        for half, totals in enumerate(self.reduce.third()):
+            for y, total in enumerate(totals):
+                self.own[half, y] = total.astype(BF)
         self.copies = []
-        for n, other in enumerate(uly_others()):
-            copy = remote(self.own, self.buf.at[n], self.send_sem.at[n], self.recv_sem.at[n], other)
+        for n, (w, core) in enumerate(self.others()):
+            copy = remote(
+                self.own.at[core], self.buf.at[self.w, self.core],
+                self.send_sem.at[n], self.recv_sem.at[self.w * 2 + self.core],
+                (blk_of(w % 2, self.z, self.x), w // 2 * 2 + core),
+            )
             copy.start()
             self.copies.append(copy)
-
-    def send(self, src, dst, n, y, z, x):
-        copy = remote(src, dst, self.all_send.at[n], self.all_recv.at[n], (blk_of(y, z, x), self.uly))
+        self.buf[self.w, self.core] = self.own[self.core]
+
+    def send(self, src, dst, n, d, e):
+        z, x = self.at(d, e)
+        copy = remote(
+            src, dst, self.all_send.at[n], self.all_recv.at[n], (blk_of(self.y, z, x), self.uly)
+        )
         copy.start()
         self.flying.append(copy)
 
-    def item(self, y, d=0, e=0):
+    def at(self, d, e):
         dz, dx = self.core * d + (1 - self.core) * e, self.core * e + (1 - self.core) * d
-        return self.all_ref.at[self.core, y, (self.z + dz) % 4, (self.x + dx) % 4]
-
-    def along(self, y, src, n, d, e):
-        dz, dx = self.core * d + (1 - self.core) * e, self.core * e + (1 - self.core) * d
-        self.send(src[0], src[1], n, self.y, (self.z + dz) % 4, (self.x + dx) % 4)
-
-    def along_first(self, y, src, first):
+        return (self.z + dz) % 4, (self.x + dx) % 4
+
+    def items(self, d=0, e=0):
+        z, x = self.at(d, e)
+        return self.all_ref.at[self.core, :, z, x]
+
+    def join(self):
+        for w, core in self.others():
+            wait_arrival(self.buf.at[w, core], self.recv_sem.at[w * 2 + core])
+        kept = self.kept
+
+        def term(w, core, y):
+            return self.buf[w, core, y].astype(F32)
+
+        for y in (0, 1):
+            for uly in range(4):
+                w, core = uly // 2 * 2, uly % 2
+                value = term(w, core, y)[:kept] + term(w + 1, core, y)[:kept]
+                self.full[y, uly * kept : (uly + 1) * kept] = value.astype(BF)
+            if self.summed:
+                self.full[y, 4 * kept :] = sum(
+                    term(w, core, y)[kept:] for w in range(4) for core in (0, 1)
+                ).astype(BF)
         for d in (1, 2, 3):
-            self.along(y, (src, self.item(y)), first + d, d, 0)
-
-    def join(self):
-        for copy in self.copies:
-            copy.wait()
-        kept = self.kept
-        terms = [self.own] + [self.buf.at[n] for n in range(3)]
-        who = [self.uly] + [other[1] for other in uly_others()]
-        for half in (0, 1):
-            for term, uly in zip(terms, who):
-                self.full[half, pl.ds(uly * kept, kept)] = term[half, :kept]
-            if self.summed:
-                self.full[half, 4 * kept :] = sum(
-                    term[half, kept:].astype(F32) for term in terms
-                ).astype(BF)
-        own = self.full.at[self.core]
-        self.send(own, self.item(self.y), 0, 1 - self.y, self.z, self.x)
-        self.along_first(self.y, own, 0)
-        self.local = pltpu.make_async_copy(own, self.item(self.y), self.local_sem)
+            self.send(self.full, self.items(), d - 1, d, 0)
+        self.local = pltpu.make_async_copy(self.full, self.items(), self.local_sem)
         self.local.start()
-
-    def onward(self):
-        other = self.item(1 - self.y)
-        wait_arrival(other, self.all_recv.at[0])
-        self.along_first(1 - self.y, other, 3)
 
     def spread(self):
         self.local.wait()
-        for k, y in enumerate((self.y, 1 - self.y)):
-            for d in range(4):
-                if d > 0:
-                    wait_arrival(self.item(y, 4 - d), self.all_recv.at[3 * k + d])
-                for e in (1, 2, 3):
-                    ref = self.item(y, (4 - d) % 4)
-                    self.along(y, (ref, ref), 7 + k * 12 + d * 3 + e - 1, 0, e)
+        for d in range(4):
+            ref = self.items((4 - d) % 4)
+            if d > 0:
+                wait_arrival(ref, self.all_recv.at[d - 1])
+            for e in (1, 2, 3):
+                self.send(ref, ref, 2 + d * 3 + e, 0, e)
 
     def hand(self):
-        for k, y in enumerate((self.y, 1 - self.y)):
-            for d in range(4):
-                for e in (1, 2, 3):
-                    wait_arrival(
-                        self.item(y, (4 - d) % 4, 4 - e), self.all_recv.at[7 + k * 12 + d * 3 + e - 1]
-                    )
+        for d in range(4):
+            for e in (1, 2, 3):
+                wait_arrival(self.items((4 - d) % 4, 4 - e), self.all_recv.at[2 + d * 3 + e])
         self.pair(self.core).start()
 
     def pair(self, core):
@@ -1507,15 +1505,14 @@
         )
 
     def end(self):
-        for copy in self.flying:
+        for copy in self.copies + self.flying:
             copy.wait_send()
         self.pair(self.core).wait_send()
         wait_arrival(self.all_ref.at[1 - self.core], self.pair_recv)
 
     def steps(self):
         return [
-            self.reduce.first, self.reduce.second, self.reduce.third, self.across, self.join,
-            self.onward, self.spread, self.hand, self.end,
+            self.reduce.first, self.reduce.second, self.across, self.join, self.spread, self.hand, self.end,
         ]
 
 
@@ -1540,7 +1537,7 @@
     result_ref, input_grad_ref, ff_all, qkv_all,
     gains_ref, total_ref, down_ref, cols_ref, ff_ref, resid_ref, cot_ref, ao_ref, mixed_ref, wo_ref, kv_ref, q_ref, limit_ref,
     lse_ref, wq_ref, rows_ref, normed_ref, b_qkv_ref, cos_ref, sin_ref, a_ref, bo_ref, dkv_ref, acc_ref, part, dq_ref, grad_ref, grad_attn, grad_resid, grad_qkv,
-    cross_out, cross_in, home_out, home_in, turned_ref, by_rows_ref, dot_ref, copy_sem, cross_sem, home_send,
+    cross_out, cross_in, home_out, home_in, turned_ref, by_rows_ref, dot_ref, back, copy_sem, cross_sem, home_send,
     home_recv, *scratch,
 ):
     y, z, x, blk, uly = place()
@@ -1575,7 +1572,11 @@
     for copy in copies:
         copy.start()
     greet(
-        reduce_others() + uly_others() + [(blk_of(1 - y, z, x), (uly + 2) % 4)] + home_from + home_to
+        reduce_others()
+        + uly_others()
+        + [(blk_of(1 - y, z, x), other[1]) for other in uly_others()]
+        + home_from
+        + home_to
     )
     collect_out = RingSum(
         lambda d: down_ref[(ring_at() + d) % 4].astype(F32), take(RingSum.scratches)
@@ -1688,8 +1689,10 @@
         backward_blocks(1, n, n + 2, *args)
         more = [shed(high, names.pop(0))] if names else []
         more += [extra.pop(0)] if extra else []
-        if n < middle - 2:
-            beside(*more)
+        for one in more:
+            one()
+        if n == 2:
+            beside()
     pack(0)
     for stream in low:
         stream.first()
@@ -1702,7 +1705,6 @@
     a_qkv = a_ref[...].reshape(48, D)
     for stream in low:
         stream.second()
-    beside()
     cos_table, sine_table = cos_ref[...], sin_ref[...]
 
     def turn_back(value, rows=slice(None)):
@@ -1720,38 +1722,41 @@
             grad_qkv[rows, group : group + HEAD] = turn_back(value[:, :HEAD], rows).astype(BF)
             grad_qkv[rows, group + HEAD :] = value[:, HEAD:].astype(BF)
 
+    latent_qkv = dot_nt(a_qkv, normed_ref[...]).astype(BF)
+
+    def project_back(slot):
+        rows = slice(slot * CHUNK, (slot + 1) * CHUNK)
+        grads = grad_qkv[rows, :]
+        lifted = dot(dot_nt(grads, b_qkv_ref[...]).astype(BF), a_qkv)
+        back[slot] = dot_nt(grads[:, :512], wq_ref[0]) + dot_nt(grads[:, 512:], wq_ref[1]) + lifted
+        latent_grad = dot_nt(b_qkv_ref[...], grads).astype(BF)
+        return dot(latent_grad, normed_ref[rows, :]), dot(latent_qkv[:, rows], grads)
+
     key_value(1, high)
     for stream in low:
         stream.third()
     send_home(0, resid_ref[...] + collect_out.third())
-    latent_qkv = dot_nt(a_qkv, normed_ref[...]).astype(BF)
+    grad_a, grad_b = project_back(1)
     for stream in low:
         stream.fourth()
     key_value(0, low)
-
-    def project_back(rows):
-        grads = grad_qkv[rows, :]
-        lifted = dot(dot_nt(grads, b_qkv_ref[...]).astype(BF), a_qkv)
-        return dot_nt(grads[:, :512], wq_ref[0]) + dot_nt(grads[:, 512:], wq_ref[1]) + lifted
-
-    cross_out[...] = project_back(other_rows).astype(BF)
+    more_a, more_b = project_back(0)
+    cross_out[...] = back[1 - h].astype(BF)
     cross = remote(cross_out, cross_in, cross_sem.at[2], cross_sem.at[3], partner)
     cross.start()
-    back_qkv = dot_nt(b_qkv_ref[...], grad_qkv[...]).astype(BF)
-    grad_b = dot(latent_qkv, grad_qkv[...])
+    grad_a, grad_b = grad_a + more_a, grad_b + more_b
     qkv_total.pack_kept(
-        units(dot(back_qkv, normed_ref[...]))
+        units(grad_a)
         + units(grad_b[:16, :group])
         + units(grad_b[16:32, group : group + HEAD])
         + units(grad_b[32:, group + HEAD :])
     )
     last_steps = qkv_total.steps()
     last_steps.pop(0)()
-    mine = project_back(own_rows)
     last_steps.pop(0)()
     beside()
     cross.wait()
-    mine = mine + cross_in[...].astype(F32)
+    mine = back[h] + cross_in[...].astype(F32)
     tokens = rows_ref[own_rows, :].astype(F32)
     send_home(1, grad_resid[...] + norm_back(tokens, norm_scale(tokens), gain(gains_ref, 0), mine))
     for step in last_steps + steps:
@@ -1812,6 +1817,7 @@
             pltpu.VMEM((2, 2, HEAD, ROWS), BF),
             pltpu.VMEM((2, 2, ROWS, HEAD), BF),
             pltpu.VMEM((2, 8, ROWS), F32),
+            pltpu.VMEM((2, CHUNK, D), F32),
             dma((22,)), dma((4,)), dma((2, 2)), dma((2, 2)),
         ]
         + RingSum.scratch()

time: 357 us -> 351 us (0.983)
  Pallas kernels: 348 us -> 342 us
    pallas_call x1, Pallas kernels: 129 us -> 123 us  [backward(): pl.pallas_call(backward_kernel, out_shape=(jax.ShapeDtypeStruct((2, CHUNK...]
where the time goes in v2:
time: 351 us; the launch traced here: 344 us
  Pallas kernels  342 us (97%)
    pallas_call x1, Pallas kernels, forward(): pl.pallas_call(forward_kernel, out_shape=(HELD((2 * CHUNK, group), BF), H...  128 us
    pallas_call x1, Pallas kernels, backward(): pl.pallas_call(backward_kernel, out_shape=(jax.ShapeDtypeStruct((2, CHUNK...  123 us
    pallas_call x1, Pallas kernels, feed_forward(): pl.pallas_call(ff_kernel, out_shape=(HELD((CHUNK, D), F32), HELD(pieces,...  79.2 us
    pallas_call x1, Pallas kernels, fold(): pl.pallas_call(fold_kernel, grid=(SETS,), out_shape=(jax.ShapeDtypeStruct...  11.6 us

profile of v2, /device:TPU:1, one launch (start us, length us, event | category | flops | bytes accessed | tf_op | source)
XLA Modules:
  0.0 344.2 jit_solution(9779003408788460392)
XLA Ops:
  0.6 1.3 maximum_bitcast_fusion.gains_hbm
  2.0 128.0 %forward.1 = (bf16[256,768]{1,0:T(8,128)(2,1)}, bf16[256,768]{1,0:T(8,128)(2,1)}, f32[2,8,768]{2,1,0:T(8,128)}, bf16[64,128,256]{2,1,0:T(8,128)(2,1)}, bf16[2,15...) custom-call(bf16[2,64,1536]{2,1,0:T(8,128)(2,1)} %tokens_ref.1, ...), custom_call_target="tpu_custom_call" | custom-call | tf_op jit(solution)/shard_map/forward/pallas_call | solution.py:813
  130.0 79.2 %feed_forward.1 = (f32[128,1536]{1,0:T(8,128)}, bf16[4,128,1536]{2,1,0:T(8,128)(2,1)}, bf16[96,2304]{1,0:T(8,128)(2,1)}, bf16[96,1536]{1,0:T(8,128)(2,1)}) custom-call(s32[2]{0:T(128)} %set_ref.3, bf16[128,1536]{1,0:T(8,128)(2,1)} %get-tuple-element.37.own_hbm, bf16[2,4,128,1536]{3,2,1,0:T(8,128)(2,1)} %get-tuple-element.38.cot_hbm, ...), custom_call_target="tpu_custom_call" | custom-call | tf_op jit(solution)/shard_map/feed_forward/pallas_call | solution.py:1137
  209.1 0.0 copy-start
  209.1 123.2 %backward.1 = (bf16[2,64,1536]{2,1,0:T(8,128)(2,1)}, bf16[2,64,1536]{2,1,0:T(8,128)(2,1)}, bf16[2,2,4,4,10,16,128]{6,5,4,3,2,1,0:T(8,128)(2,1)}, bf16[2,2,4,4,4,16,128]{6,5,4,3,2,1,0:T(8,128)(2,1)}) custom-call(f32[40,128]{1,0:T(8,128)} %maximum_bitcast_fusion.gains_hbm, f32[128,1536]{1,0:T(8,128)} %get-tuple-element.42.total_hbm, ...), custom_call_target="tpu_custom_call" | custom-call | tf_op jit(solution)/shard_map/backward/pallas_call | solution.py:1772
  332.3 0.0 copy-done
  332.4 11.6 %fold.1 = (bf16[2,64,1536]{2,1,0:T(8,128)(2,1)}, f32[2,64,1536]{2,1,0:T(8,128)}, f32[6,8,16,1536]{3,2,1,0:T(8,128)}, f32[8,16,8960]{2,1,0:T(8,128)}, f32[3,8,16,...) custom-call(s32[2]{0:T(128)S(1)} %copy-done, ...), custom_call_target="tpu_custom_call" | custom-call | tf_op jit(solution)/shard_map/fold/pallas_call | solution.py:1928
Async XLA Ops:
  209.1 123.2 %copy-start = (s32[2]{0:T(128)S(1)}, s32[2]{0:T(128)}, u32[]{:S(2)}) copy-start(s32[2]{0:T(128)} %set_ref.3) | copy-start | bytes 28
